TPU v7x, 256 devices: a whole 4x4x8 slice. The times are simulated.
256 devices in a mesh: clus: 32 (over x, z), pair: 8 (over y, core).
Axes of the slice: x: 4, y: 4, z: 8, core: 2. Of those that a mesh axis runs over, the one named last changes fastest.
Arguments:
- child_basis: float32 [256, 256, 256], P('clus'), as said below
- transfer: float32 [256, 256, 256], P('clus'), may hold values from -0.5 to 0.5
- child_parent: int32 [32, 8], P('clus'), may hold values from 0 to 1, never falling along the last dimension, each value on 1 to 6 neighbouring positions
- upper_weight: float32 [64, 256, 256], P('clus'), as said below
- child_pairs: int32 [3072, 2], P(('clus', 'pair')), may hold values from -1 to 255, as said below
- child_blocks: float32 [3072, 256, 256], P(('clus', 'pair')), may hold values from -0.15625 to 0.15625
- parent_pairs: int32 [2048, 2], P(('clus', 'pair')), may hold values from -1 to 63, as said below
- parent_blocks: float32 [2048, 256, 256], P(('clus', 'pair')), may hold values from -0.15625 to 0.15625
Outputs:
- child_weight: float32 [256, 256, 256], P('clus')
- parent_basis: float32 [64, 256, 256], P('clus')
Inputs may be any that keep to these rules, and one draw needn't show every extreme that they name: `child_pairs`: each device's aligned block of 12 rows holds its valid pairs first and then rows of -1, -1; every block has one valid row or more and some block is full. In the block of flat device index d (clus index c = d // 8), box i lies among the 8 boxes of clus index c, box j among those of clus indices c to c + 3, and j differs from i. `parent_pairs`: as for child_pairs, with blocks of 8 rows and the 2 parent boxes of each clus index. `child_basis`: symmetric positive definite. `upper_weight`: symmetric positive definite.
All inputs are finite; a program needn't handle non-finite values.
Results may differ from a plain program's by a relative error of at most 0.0003.
Values sent between devices are 32-bit elements; how exact they have to be, the bound alone decides.
No kernel may reach another device: no remote copies, remote signals or barrier semaphores. Data moves between devices by JAX's collectives and lax.ppermute only.
A program may use at most 128 MiB of HBM per device.

v0:
```python
import functools

import jax
import jax.numpy as jnp
from jax import lax
from jax.experimental import pallas as pl
from jax.experimental.pallas import tpu as pltpu
from jax.sharding import PartitionSpec as P

REACH = 3
PAIR = 8
HALF = 128
PART = 256
DIAG = 320
SHARE = 328
UNROLL = 4
PARENTS = 2
CHILD_LIST = 10
PARENT_LIST = 34
VMEM_LIMIT = 24 * 2**20

NN = (((1,), (0,)), ((), ()))
NT = (((1,), (1,)), ((), ()))
TN = (((0,), (0,)), ((), ()))

VMEM = pl.BlockSpec(memory_space=pltpu.VMEM)
SMEM = pl.BlockSpec(memory_space=pltpu.SMEM)
ANY = pl.BlockSpec(memory_space=pl.ANY)


def split(value):
    high = value.astype(jnp.bfloat16)
    return high, (value - high.astype(jnp.float32)).astype(jnp.bfloat16)


def product(left, right, dims):
    def one(a, b):
        return lax.dot_general(a, b, dims, preferred_element_type=jnp.float32)

    return one(left[0], right[0]) + (one(left[0], right[1]) + one(left[1], right[0]))


def inner(blocks, grams):
    blocks = [split(block) for block in blocks]
    grams = [split(gram) for gram in grams]
    halfway = [split(product(gram, block, NN)) for gram, block in zip(grams, blocks)]
    return [product(block, value, TN) for block, value in zip(blocks, halfway)]


def outer(blocks, grams):
    blocks = [split(block) for block in blocks]
    grams = [split(gram) for gram in grams]
    halfway = [split(product(block, gram, NN)) for gram, block in zip(grams, blocks)]
    return [product(value, block, NT) for block, value in zip(blocks, halfway)]


def each(count, body):
    lax.fori_loop(0, count, lambda i, carry: (body(i), carry)[1], 0)


def cleared(ref):
    def clear(i):
        ref[i] = jnp.zeros(ref.shape[1:], ref.dtype)

    each(ref.shape[0], clear)


def grids():
    rows = lax.broadcasted_iota(jnp.int32, (HALF, HALF), 0)
    cols = lax.broadcasted_iota(jnp.int32, (HALF, HALF), 1)
    return rows, cols


def packed(full):
    rows, cols = grids()
    first, last = full[:HALF, :HALF], full[HALF:, HALF:]
    diagonal = jnp.sum(jnp.where(rows == cols, first, 0.0), axis=0, keepdims=True)
    return full[HALF:, :HALF], jnp.where(rows > cols, first, last), diagonal


def packed_sum(half):
    rows, cols = grids()
    first, last = half[:HALF, :HALF], half[HALF:, HALF:]
    diagonal = jnp.sum(jnp.where(rows == cols, 2.0 * first, 0.0), axis=0, keepdims=True)
    lower = half[HALF:, :HALF] + half[:HALF, HALF:].T
    both = jnp.where(rows > cols, first, last) + jnp.where(rows < cols, first, last).T
    return lower, both, diagonal


def halved(lower, both, diagonal):
    rows, cols = grids()
    zero = jnp.zeros((HALF, HALF), jnp.float32)
    first = jnp.where(rows > cols, both, jnp.where(rows == cols, 0.5 * diagonal, 0.0))
    last = jnp.where(rows < cols, both, jnp.where(rows == cols, 0.5 * both, 0.0))
    return jnp.concatenate(
        [jnp.concatenate([first, zero], axis=1), jnp.concatenate([lower, last], axis=1)], axis=0
    )


def place_of(box, me):
    return ((box ^ me) & 1) * 4 + (((box >> 1) - (me >> 1)) & 3)


def box_at(place, me):
    return ((((place & 3) + (me >> 1)) & 3) << 1) | ((place >> 2) ^ (me & 1))


def lift_kernel(
    where, basis_in, transfer_in, parent_basis, own_same, own_other, share,
    basis, transfer, rows_of_parents, sems,
):
    me = where[1]
    count = basis.shape[0] // UNROLL

    def copies(group):
        at = pl.ds(group * UNROLL, UNROLL)
        return [
            pltpu.make_async_copy(basis_in.at[at], basis.at[at], sems.at[0, group]),
            pltpu.make_async_copy(transfer_in.at[at], transfer.at[at], sems.at[1, group]),
        ]

    for group in range(count):
        for copy in copies(group):
            copy.start()
    cleared(parent_basis)

    def lift(group):
        for copy in copies(group):
            copy.wait()
        children = [group * UNROLL + step for step in range(UNROLL)]
        terms = inner([transfer[c] for c in children], [basis[c] for c in children])
        for child, term in zip(children, terms):
            parent_basis[where[PARENTS + child]] += term

    each(count, lift)
    diagonals = []
    for parent in range(2):
        lower, both, diagonal = packed(parent_basis[parent])
        rows_of_parents[parent * 256 : parent * 256 + HALF] = lower
        rows_of_parents[parent * 256 + HALF : parent * 256 + 256] = both
        diagonals.append(diagonal)
    for own, first in ((own_same, 0), (own_other, 4)):

        def pack(at):
            box = box_at(first + at, me)
            lower, both, diagonal = packed(basis[box])
            own[at, :HALF] = lower
            own[at, HALF:PART] = both
            own[at, PART:DIAG] = rows_of_parents[pl.ds(pl.multiple_of(box * 64, 64), 64)]
            own[at, DIAG:] = jnp.concatenate(
                [diagonal, *diagonals, jnp.zeros((SHARE - DIAG - 3, HALF), jnp.float32)], axis=0
            )

        each(4, pack)
    share[...] = own_same[0]


def far_kernel(
    where, child_basis, parent_basis, child_blocks, parent_blocks, kept, sent, own, total,
):
    clus, me = where[0], where[1]
    child_groups = child_blocks.shape[0] // UNROLL
    parent_groups = parent_blocks.shape[0] // UNROLL
    cleared(total)
    trash = 4 * PAIR

    def of_children(group):
        rows = [group * UNROLL + step for step in range(UNROLL)]
        nears = [where[CHILD_LIST + 2 * row] for row in rows]
        grams = [child_basis[jnp.where(near >= 0, near - clus * PAIR, 0)] for near in nears]
        for row, term in zip(rows, inner([child_blocks[row] for row in rows], grams)):
            lower, both, diagonal = packed(term)
            far = where[CHILD_LIST + 2 * row + 1]
            slot = place_of(far & 7, me) * 4 + (far >> 3) - clus
            slot = jnp.where(far >= 0, slot, trash)
            total[slot, :HALF] += lower
            total[slot, HALF:PART] += both
            total[slot, DIAG : DIAG + 1] += diagonal

    def of_parents(group):
        rows = [group * UNROLL + step for step in range(UNROLL)]
        nears = [where[PARENT_LIST + 2 * row] for row in rows]
        grams = [parent_basis[jnp.where(near >= 0, near - clus * 2, 0)] for near in nears]
        blocks = [parent_blocks[row] for row in rows]
        for row, term in zip(rows, inner(blocks, grams)):
            lower, both, diagonal = packed(term)
            far = where[PARENT_LIST + 2 * row + 1]
            usable = far >= 0
            offset, parent = (far >> 1) - clus, far & 1
            pieces = (lower[:64], lower[64:], both[:64], both[64:])
            for piece, lines in enumerate(pieces):
                slot = place_of(parent * 4 + piece, me) * 4 + offset
                total[jnp.where(usable, slot, trash), PART:DIAG] += lines
            slot = jnp.where(usable, place_of(0, me) * 4 + offset, trash)
            lines = lax.broadcasted_iota(jnp.int32, (8, HALF), 0)
            total[slot, DIAG:] += jnp.where(lines == parent + 1, diagonal, 0.0)

    each(child_groups, of_children)
    each(parent_groups, of_parents)
    for target, first_place in ((kept, 0), (sent, 4)):

        def hand_out(at):
            place = first_place + at
            own[place] = total[place * 4]
            for offset in range(REACH):
                target[at, offset] = total[place * 4 + 1 + offset]

        each(4, hand_out)


def near_kernel(
    where, after, also_after, child_blocks, parent_blocks, own_terms, own_same, own_other, first, other_first,
    *rest,
):
    pieces = rest[: 2 * PAIR]
    kept, sent, window, total, rows_of_parents = rest[2 * PAIR :]
    clus, me = where[0], where[1]
    halves = ((own_same, 0, 0), (own_other, 4, 0), (first, 0, 1), (other_first, 4, 1))
    for source, first_place, offset in halves:

        def take_half(at):
            window[first_place + at, offset] = source[at]

        each(4, take_half)
    for i, piece in enumerate(pieces):
        window[i % PAIR, 2 + i // PAIR] = piece[...]
    child_groups = child_blocks.shape[0] // UNROLL
    parent_groups = parent_blocks.shape[0] // UNROLL
    cleared(total)
    trash = PAIR + 2

    def of_children(group):
        rows = [group * UNROLL + step for step in range(UNROLL)]
        grams = []
        for row in rows:
            far = where[CHILD_LIST + 2 * row + 1]
            place = place_of(far & 7, me)
            offset = jnp.where(far >= 0, (far >> 3) - clus, 0)
            grams.append(
                halved(
                    window[place, offset, :HALF],
                    window[place, offset, HALF:PART],
                    window[place, offset, DIAG : DIAG + 1],
                )
            )
        for row, term in zip(rows, outer([child_blocks[row] for row in rows], grams)):
            near = where[CHILD_LIST + 2 * row]
            total[jnp.where(near >= 0, near - clus * PAIR, trash)] += term

    def of_parents(group):
        rows = [group * UNROLL + step for step in range(UNROLL)]
        grams = []
        for row in rows:
            far = where[PARENT_LIST + 2 * row + 1]
            parent = far & 1
            offset = jnp.where(far >= 0, (far >> 1) - clus, 0)
            lines = [
                window[place_of(parent * 4 + piece, me), offset, PART:DIAG] for piece in range(4)
            ]
            diagonals = window[0, offset, DIAG:]
            grams.append(
                halved(
                    jnp.concatenate(lines[:2], axis=0),
                    jnp.concatenate(lines[2:], axis=0),
                    jnp.where(parent == 0, diagonals[1:2], diagonals[2:3]),
                )
            )
        blocks = [parent_blocks[row] for row in rows]
        for row, term in zip(rows, outer(blocks, grams)):
            near = where[PARENT_LIST + 2 * row]
            total[jnp.where(near >= 0, PAIR + near - clus * 2, trash)] += term

    each(child_groups, of_children)
    each(parent_groups, of_parents)
    diagonals = []
    for parent in range(2):
        lower, both, diagonal = packed_sum(total[PAIR + parent])
        rows_of_parents[parent * 256 : parent * 256 + HALF] = lower
        rows_of_parents[parent * 256 + HALF : parent * 256 + 256] = both
        diagonals.append(diagonal)
    for target, first_place in ((kept, 0), (sent, 4)):

        def pack(at):
            place = first_place + at
            box = box_at(place, me)
            lower, both, diagonal = packed_sum(total[box])
            target[at, :HALF] = own_terms[place, :HALF] + lower
            target[at, HALF:PART] = own_terms[place, HALF:PART] + both
            target[at, PART:DIAG] = (
                own_terms[place, PART:DIAG]
                + rows_of_parents[pl.ds(pl.multiple_of(box * 64, 64), 64)]
            )
            lines = [jnp.where(box == 0, line, 0.0) for line in diagonals]
            target[at, DIAG:] = own_terms[place, DIAG:] + jnp.concatenate(
                [diagonal, *lines, jnp.zeros((SHARE - DIAG - 3, HALF), jnp.float32)], axis=0
            )

        each(4, pack)


def lower_kernel(where, transfer, upper, *rest):
    pieces, weight, shares, coarse = rest[:PAIR], *rest[PAIR:]
    me = where[1]
    for place in range(PAIR):
        shares[place] = pieces[place][...]
    diagonals = shares[place_of(0, me), DIAG:]
    for parent in range(2):
        rows = [shares[place_of(parent * 4 + piece, me), PART:DIAG] for piece in range(4)]
        coarse[parent] = 0.5 * upper[parent] + halved(
            jnp.concatenate(rows[:2], axis=0),
            jnp.concatenate(rows[2:], axis=0),
            diagonals[parent + 1 : parent + 2],
        )

    def lower(group):
        children = [group * UNROLL + step for step in range(UNROLL)]
        terms = outer(
            [transfer[child] for child in children],
            [coarse[where[PARENTS + child]] for child in children],
        )
        for child, term in zip(children, terms):
            place = place_of(child, me)
            term = term + halved(
                shares[place, :HALF], shares[place, HALF:PART], shares[place, DIAG : DIAG + 1]
            )
            weight[child] = term + term.T

    each(weight.shape[0] // UNROLL, lower)


def call(kernel, name, out_shape, in_specs, out_specs, scratch, products):
    return pl.pallas_call(
        kernel,
        name=name,
        out_shape=out_shape,
        in_specs=in_specs,
        out_specs=out_specs,
        scratch_shapes=scratch,
        compiler_params=pltpu.CompilerParams(vmem_limit_bytes=VMEM_LIMIT),
        cost_estimate=pl.CostEstimate(
            flops=products * 6 * 256**3, bytes_accessed=8 * 2**20, transcendentals=0
        ),
    )


def floats(*shape):
    return jax.ShapeDtypeStruct(shape, jnp.float32)


def to_clus(value, steps):
    count = lax.axis_size("clus")
    return lax.ppermute(value, "clus", [(i, (i + steps) % count) for i in range(count)])


def to_y(value, steps):
    return lax.ppermute(value, "pair", [(i, (i + 2 * steps) % PAIR) for i in range(PAIR)])


def to_core(value):
    return lax.ppermute(value, "pair", [(i, i ^ 1) for i in range(PAIR)])


def everywhere(share):
    pieces = [share] + [to_y(share, -step) for step in range(1, 4)]
    return pieces + [to_core(piece) for piece in pieces]


def per_device(
    child_basis,
    transfer,
    child_parent,
    upper_weight,
    child_pairs,
    child_blocks,
    parent_pairs,
    parent_blocks,
):
    boxes, extent = child_basis.shape[0], child_basis.shape[-1]
    where = jnp.concatenate(
        [
            jnp.stack([lax.axis_index("clus"), lax.axis_index("pair")]).astype(jnp.int32),
            child_parent.reshape(-1),
            child_pairs.reshape(-1),
            parent_pairs.reshape(-1),
        ]
    )

    parent_basis, own_same, own_other, share = call(
        lift_kernel,
        "lift",
        (
            floats(2, extent, extent),
            floats(4, SHARE, HALF),
            floats(4, SHARE, HALF),
            floats(SHARE, HALF),
        ),
        [SMEM, ANY, ANY],
        (VMEM, VMEM, VMEM, VMEM),
        [
            pltpu.VMEM((boxes, extent, extent), jnp.float32),
            pltpu.VMEM((boxes, extent, extent), jnp.float32),
            pltpu.VMEM((512, HALF), jnp.float32),
            pltpu.SemaphoreType.DMA((2, boxes // UNROLL)),
        ],
        16,
    )(where, child_basis, transfer)

    second = to_clus(share, -2)

    kept, sent, own_terms = call(
        far_kernel,
        "far",
        (
            floats(4, REACH, SHARE, HALF),
            floats(4, REACH, SHARE, HALF),
            floats(PAIR, SHARE, HALF),
        ),
        [SMEM, VMEM, VMEM, VMEM, VMEM],
        (VMEM, VMEM, VMEM),
        [
            pltpu.VMEM((4 * PAIR + 1, SHARE, HALF), jnp.float32),
        ],
        40,
    )(where, child_basis, parent_basis, child_blocks, parent_blocks)

    second, own_same, kept, sent = lax.optimization_barrier((second, own_same, kept, sent))
    barrier = lax.optimization_barrier
    third = to_clus(second, -1)
    got = to_core(sent)
    seconds = [second] + [to_y(second, -step) for step in range(1, 4)]
    third, got, seconds = barrier((third, got, seconds))

    first = to_clus(own_same, -1)
    far_first = to_clus(kept[:, 0] + got[:, 0], 1)
    parts = [kept[step, 1:] + got[step, 1:] for step in range(4)]
    received = [to_y(parts[step], step) for step in range(1, 4)]
    first, far_first, received, third, seconds = barrier(
        (first, far_first, received, third, seconds)
    )

    far_sum = parts[0] + received[0] + received[1] + received[2]
    far_third = to_clus(far_sum[1], 1)
    thirds = [third] + [to_y(third, -step) for step in range(1, 4)]
    other_first = to_core(first)
    far_third, thirds, other_first, seconds = barrier((far_third, thirds, other_first, seconds))

    far_later = to_clus(far_sum[0] + far_third, 2)
    second_pieces = seconds + [to_core(piece) for piece in seconds]
    third_pieces = thirds + [to_core(piece) for piece in thirds]

    kept, sent = call(
        near_kernel,
        "near",
        (floats(4, SHARE, HALF), floats(4, SHARE, HALF)),
        [SMEM, ANY, ANY, VMEM, VMEM, VMEM] + [VMEM] * (2 * PAIR + 4),
        (VMEM, VMEM),
        [
            pltpu.VMEM((PAIR, REACH + 1, SHARE, HALF), jnp.float32),
            pltpu.VMEM((PAIR + 3, extent, extent), jnp.float32),
            pltpu.VMEM((512, HALF), jnp.float32),
        ],
        40,
    )(
        where, far_third, far_first, child_blocks, parent_blocks, own_terms, own_same, own_other,
        first, other_first, *second_pieces, *third_pieces,
    )

    kept, sent, far_later = lax.optimization_barrier((kept, sent, far_later))
    got = to_core(sent)
    parts = [kept[step] + got[step] + far_first[step] for step in range(4)]
    total = parts[0] + far_later
    for step in range(1, 4):
        total = total + to_y(parts[step], step)

    child_weight = call(
        lower_kernel,
        "lower",
        floats(boxes, extent, extent),
        [SMEM, VMEM, VMEM] + [VMEM] * PAIR,
        VMEM,
        [
            pltpu.VMEM((PAIR, SHARE, HALF), jnp.float32),
            pltpu.VMEM((2, extent, extent), jnp.float32),
        ],
        16,
    )(where, transfer, upper_weight, *everywhere(total))
    return child_weight, parent_basis


def solution(mesh):
    return jax.shard_map(
        per_device,
        mesh=mesh,
        in_specs=(
            P("clus", None, None),
            P("clus", None, None),
            P("clus", None),
            P("clus", None, None),
            P(("clus", "pair"), None),
            P(("clus", "pair"), None, None),
            P(("clus", "pair"), None),
            P(("clus", "pair"), None, None),
        ),
        out_specs=(P("clus", None, None), P("clus", None, None)),
        check_vma=False,
    )
```

profile of v0, /device:TPU:1, one launch (start us, length us, event | category | flops | bytes accessed | tf_op | source)
XLA Modules:
  0.0 127.7 jit_solution(966599502432030958)
XLA Ops:
  0.6 0.8 copy.12
  1.5 0.8 copy.13
  2.3 0.7 concatenate.3.where
  3.1 1.6 %copy-done = f32[8,256,256]{2,1,0:T(8,128)S(1)} copy-done((f32[8,256,256]{2,1,0:T(8,128)S(1)}, f32[8,256,256]{2,1,0:T(8,128)}, u32[]{:S(2)}) %copy-start) | copy-done | bytes 2097176
  4.7 1.6 %copy-done.4 = f32[8,256,256]{2,1,0:T(8,128)S(1)} copy-done((f32[8,256,256]{2,1,0:T(8,128)S(1)}, f32[8,256,256]{2,1,0:T(8,128)}, u32[]{:S(2)}) %copy-start.4) | copy-done | bytes 2097176
  6.3 4.0 %lift.1 = (f32[2,256,256]{2,1,0:T(8,128)}, f32[4,328,128]{2,1,0:T(8,128)S(1)}, f32[4,328,128]{2,1,0:T(8,128)S(1)}, f32[328,128]{1,0:T(8,128)S(1)}) custom-call(s32[50]{0:T(128)S(1)} %concatenate.3.where, f32[8,256,256]{2,1,0:T(8,128)S(1)} %copy-done.4, f32[8,256,256]{2,1,0:T(8,128)S(1)} %copy-done), custom_call_target="tpu_custom_call" | custom-call | flops 1610612736 | bytes 8388608 | tf_op jit(solution)/shard_map/lift/pallas_call | solution.py:388
  10.3 9.1 %collective-permute-start = (f32[328,128]{1,0:T(8,128)S(1)}, f32[328,128]{1,0:T(8,128)S(1)}, u32[]{:S(2)}, u32[]{:S(2)}) collective-permute-start(f32[328,128]{1,0:T(8,128)S(1)} %get-tuple-element.44), channel_id=1, source_target_pairs={{0,240},{8,248},{16,0},{24,8},{32,16},{40,24},{48,32},{56,40},{64,... | collective-permute-start | bytes 503816 | tf_op jit(solution)/shard_map/ppermute | solution.py:352
  19.4 1.0 copy-done.6
  20.5 6.7 %far.1 = (f32[4,3,328,128]{3,2,1,0:T(8,128)S(1)}, f32[4,3,328,128]{3,2,1,0:T(8,128)S(1)}, f32[8,328,128]{2,1,0:T(8,128)S(1)}) custom-call(s32[50]{0:T(128)S(1)} %concatenate.3.where, f32[8,256,256]{2,1,0:T(8,128)S(1)} %copy-done.4, f32[2,256,256]{2,1,0:T(8,128)S(1)} %copy-done.6, f32[12,256,256]{2,1,0:T(8,128)S(1)} %copy-done.3, f32[8,256,256]{2,1,0:T(8,128)S(1)} %copy-done.5), custom_call_target="tpu_custom_call" | custom-call | flops 4026531840 | bytes 8388608 | tf_op jit(solution)/shard_map/far/pallas_call | solution.py:410
  27.2 1.0 collective-permute-start.2
  28.2 3.0 %collective-permute-start.1 = (f32[328,128]{1,0:T(8,128)S(1)}, f32[328,128]{1,0:T(8,128)S(1)}, u32[]{:S(2)}, u32[]{:S(2)}) collective-permute-start(f32[328,128]{1,0:T(8,128)S(1)} %collective-permute-done.rest_0_), channel_id=1, source_target_pairs={{0,248},{8,0},{16,8},{24,16},{32,24},{40,32},{48,40},{56,48},{64,5... | collective-permute-start | bytes 503816 | tf_op jit(solution)/shard_map/ppermute | solution.py:352
  31.2 2.7 %collective-permute-start.3 = (f32[328,128]{1,0:T(8,128)S(1)}, f32[328,128]{1,0:T(8,128)S(1)}, u32[]{:S(2)}, u32[]{:S(2)}) collective-permute-start(f32[328,128]{1,0:T(8,128)S(1)} %collective-permute-done.rest_0_), channel_id=1, source_target_pairs={{0,6},{1,7},{2,0},{3,1},{4,2},{5,3},{6,4},{7,5},{8,14},{9,15},{10,... | collective-permute-start | bytes 503816 | tf_op jit(solution)/shard_map/ppermute | solution.py:356
  34.0 0.3 collective-permute-start.4
  34.3 0.7 collective-permute-start.5
  35.0 5.5 %collective-permute-start.6 = (f32[4,328,128]{2,1,0:T(8,128)S(1)}, f32[4,328,128]{2,1,0:T(8,128)S(1)}, u32[]{:S(2)}, u32[]{:S(2)}) collective-permute-start(f32[4,328,128]{2,1,0:T(8,128)S(1)} %get-tuple-element.53.own_same), channel_id=1, source_target_pairs={{0,248},{8,0},{16,8},{24,16},{32,24},{40,32},{48,40},{56,48},{64,5... | collective-permute-start | bytes 2015240 | tf_op jit(solution)/shard_map/ppermute | solution.py:352
  40.5 0.4 collective-permute-done.3.rest_1_
  40.8 4.5 %collective-permute-done.5.rest_3_ = f32[328,128]{1,0:T(8,128)S(1)} collective-permute-done((f32[328,128]{1,0:T(8,128)S(1)}, f32[328,128]{1,0:T(8,128)S(1)}, u32[]{:S(2)}, u32[]{:S(2)}) %collective-permute-start.5) | collective-permute-done | bytes 167968 | tf_op jit(solution)/shard_map/ppermute | solution.py:356
  45.3 0.1 add_bitcast_fusion
  45.5 0.1 add_bitcast_fusion.1
  45.7 1.5 %collective-permute-start.8 = (f32[2,328,128]{2,1,0:T(8,128)S(1)}, f32[2,328,128]{2,1,0:T(8,128)S(1)}, u32[]{:S(2)}, u32[]{:S(2)}) collective-permute-start(f32[2,328,128]{2,1,0:T(8,128)S(1)} %get-tuple-element.88), channel_id=1, source_target_pairs={{0,2},{1,3},{2,4},{3,5},{4,6},{5,7},{6,0},{7,1},{8,10},{9,11},{10,... | collective-permute-start | bytes 1007624 | tf_op jit(solution)/shard_map/ppermute | solution.py:356
  47.1 0.3 collective-permute-start.9
  47.5 6.6 %collective-permute-done.6.first = f32[4,328,128]{2,1,0:T(8,128)S(1)} collective-permute-done((f32[4,328,128]{2,1,0:T(8,128)S(1)}, f32[4,328,128]{2,1,0:T(8,128)S(1)}, u32[]{:S(2)}, u32[]{:S(2)}) %collective-permute-start.6) | collective-permute-done | bytes 671776 | tf_op jit(solution)/shard_map/ppermute | solution.py:352
  54.1 0.5 collective-permute-done.10
  54.6 1.4 %collective-permute-done.8 = f32[2,328,128]{2,1,0:T(8,128)S(1)} collective-permute-done((f32[2,328,128]{2,1,0:T(8,128)S(1)}, f32[2,328,128]{2,1,0:T(8,128)S(1)}, u32[]{:S(2)}, u32[]{:S(2)}) %collective-permute-start.8) | collective-permute-done | bytes 335904 | tf_op jit(solution)/shard_map/ppermute | solution.py:356
  56.0 5.9 %collective-permute-done.9 = f32[2,328,128]{2,1,0:T(8,128)S(1)} collective-permute-done((f32[2,328,128]{2,1,0:T(8,128)S(1)}, f32[2,328,128]{2,1,0:T(8,128)S(1)}, u32[]{:S(2)}, u32[]{:S(2)}) %collective-permute-start.9) | collective-permute-done | bytes 335904 | tf_op jit(solution)/shard_map/ppermute | solution.py:356
  61.9 3.0 %collective-permute-done.7.also_after = f32[4,328,128]{2,1,0:T(8,128)S(1)} collective-permute-done((f32[4,328,128]{2,1,0:T(8,128)S(1)}, f32[4,328,128]{2,1,0:T(8,128)S(1)}, u32[]{:S(2)}, u32[]{:S(2)}) %collective-permute-start.7) | collective-permute-done | bytes 671776 | tf_op jit(solution)/shard_map/ppermute | solution.py:352
  65.0 1.3 %collective-permute-start.15 = (f32[4,328,128]{2,1,0:T(8,128)S(1)}, f32[4,328,128]{2,1,0:T(8,128)S(1)}, u32[]{:S(2)}, u32[]{:S(2)}) collective-permute-start(f32[4,328,128]{2,1,0:T(8,128)S(1)} %collective-permute-done.6.first), channel_id=1, source_target_pairs={{0,1},{1,0},{2,3},{3,2},{4,5},{5,4},{6,7},{7,6},{8,9},{9,8},{10,11... | collective-permute-start | bytes 2015240 | tf_op jit(solution)/shard_map/ppermute | solution.py:360
  66.3 0.1 fusion.1
  66.4 0.3 collective-permute-start.11
  66.8 0.4 collective-permute-start.13
  67.2 1.0 collective-permute-start.14
  68.2 7.7 %collective-permute-done.11.after = f32[328,128]{1,0:T(8,128)S(1)} collective-permute-done((f32[328,128]{1,0:T(8,128)S(1)}, f32[328,128]{1,0:T(8,128)S(1)}, u32[]{:S(2)}, u32[]{:S(2)}) %collective-permute-start.11) | collective-permute-done | bytes 167968 | tf_op jit(solution)/shard_map/ppermute | solution.py:352
  75.9 2.3 %collective-permute-done.14.rest_11_ = f32[328,128]{1,0:T(8,128)S(1)} collective-permute-done((f32[328,128]{1,0:T(8,128)S(1)}, f32[328,128]{1,0:T(8,128)S(1)}, u32[]{:S(2)}, u32[]{:S(2)}) %collective-permute-start.14) | collective-permute-done | bytes 167968 | tf_op jit(solution)/shard_map/ppermute | solution.py:356
  78.2 0.5 collective-permute-start.16
  78.7 0.5 collective-permute-start.18
  79.2 0.5 collective-permute-start.20
  79.7 0.4 collective-permute-start.21
  80.1 0.2 collective-permute-start.22
  80.3 0.3 collective-permute-start.23
  80.7 0.1 collective-permute-done.20.rest_12_
  80.8 0.3 collective-permute-done.21.rest_13_
  81.1 0.4 collective-permute-done.22.rest_14_
  81.5 0.2 collective-permute-done.23.rest_15_
  81.7 7.5 %near.1 = (f32[4,328,128]{2,1,0:T(8,128)S(1)}, f32[4,328,128]{2,1,0:T(8,128)S(1)}) custom-call(s32[50]{0:T(128)S(1)} %concatenate.3.where, f32[328,128]{1,0:T(8,128)S(1)} %collective-permute-done.11.after, f32[4,328,128]{2,1,0:T(8,128)S(1)} %collective-permute-done.7.also_after, f32[12,256,256]{2,1,0:T(8,128)S(1)} %copy-done.3, ...), custom_call_target="tpu_custom_call" | custom-call | flops 4026531840 | bytes 8388608 | tf_op jit(solution)/shard_map/near/pallas_call | solution.py:451
  89.3 4.9 %collective-permute-done.24 = f32[328,128]{1,0:T(8,128)S(1)} collective-permute-done((f32[328,128]{1,0:T(8,128)S(1)}, f32[328,128]{1,0:T(8,128)S(1)}, u32[]{:S(2)}, u32[]{:S(2)}) %collective-permute-start.24) | collective-permute-done | bytes 167968 | tf_op jit(solution)/shard_map/ppermute | solution.py:352
  94.2 1.0 collective-permute-start.25
  95.3 1.7 %collective-permute-done.25 = f32[4,328,128]{2,1,0:T(8,128)S(1)} collective-permute-done((f32[4,328,128]{2,1,0:T(8,128)S(1)}, f32[4,328,128]{2,1,0:T(8,128)S(1)}, u32[]{:S(2)}, u32[]{:S(2)}) %collective-permute-start.25) | collective-permute-done | bytes 671776 | tf_op jit(solution)/shard_map/ppermute | solution.py:360
  97.0 0.1 fusion.7
  97.2 2.0 %collective-permute-start.27 = (f32[328,128]{1,0:T(8,128)S(1)}, f32[328,128]{1,0:T(8,128)S(1)}, u32[]{:S(2)}, u32[]{:S(2)}) collective-permute-start(f32[328,128]{1,0:T(8,128)S(1)} %get-tuple-element.91), channel_id=1, source_target_pairs={{0,4},{1,5},{2,6},{3,7},{4,0},{5,1},{6,2},{7,3},{8,12},{9,13},{10,... | collective-permute-start | bytes 503816 | tf_op jit(solution)/shard_map/ppermute | solution.py:356
  99.2 0.7 collective-permute-start.28
  99.9 4.7 %collective-permute-done.26 = f32[328,128]{1,0:T(8,128)S(1)} collective-permute-done((f32[328,128]{1,0:T(8,128)S(1)}, f32[328,128]{1,0:T(8,128)S(1)}, u32[]{:S(2)}, u32[]{:S(2)}) %collective-permute-start.26) | collective-permute-done | bytes 167968 | tf_op jit(solution)/shard_map/ppermute | solution.py:356
  104.6 2.3 %collective-permute-done.27 = f32[328,128]{1,0:T(8,128)S(1)} collective-permute-done((f32[328,128]{1,0:T(8,128)S(1)}, f32[328,128]{1,0:T(8,128)S(1)}, u32[]{:S(2)}, u32[]{:S(2)}) %collective-permute-start.27) | collective-permute-done | bytes 167968 | tf_op jit(solution)/shard_map/ppermute | solution.py:356
  106.8 1.0 collective-permute-done.28
  107.8 0.1 fusion.13.rest_0_
  107.9 2.8 %collective-permute-start.29 = (f32[328,128]{1,0:T(8,128)S(1)}, f32[328,128]{1,0:T(8,128)S(1)}, u32[]{:S(2)}, u32[]{:S(2)}) collective-permute-start(f32[328,128]{1,0:T(8,128)S(1)} %fusion.13.rest_0_), channel_id=1, source_target_pairs={{0,6},{1,7},{2,0},{3,1},{4,2},{5,3},{6,4},{7,5},{8,14},{9,15},{10,... | collective-permute-start | bytes 503816 | tf_op jit(solution)/shard_map/ppermute | solution.py:356
  110.7 0.7 collective-permute-start.31
  111.4 1.4 %collective-permute-start.32 = (f32[328,128]{1,0:T(8,128)S(1)}, f32[328,128]{1,0:T(8,128)S(1)}, u32[]{:S(2)}, u32[]{:S(2)}) collective-permute-start(f32[328,128]{1,0:T(8,128)S(1)} %fusion.13.rest_0_), channel_id=1, source_target_pairs={{0,1},{1,0},{2,3},{3,2},{4,5},{5,4},{6,7},{7,6},{8,9},{9,8},{10,11... | collective-permute-start | bytes 503816 | tf_op jit(solution)/shard_map/ppermute | solution.py:360
  112.8 4.7 %collective-permute-done.29.rest_1_ = f32[328,128]{1,0:T(8,128)S(1)} collective-permute-done((f32[328,128]{1,0:T(8,128)S(1)}, f32[328,128]{1,0:T(8,128)S(1)}, u32[]{:S(2)}, u32[]{:S(2)}) %collective-permute-start.29) | collective-permute-done | bytes 167968 | tf_op jit(solution)/shard_map/ppermute | solution.py:356
  117.4 1.4 %collective-permute-start.33 = (f32[328,128]{1,0:T(8,128)S(1)}, f32[328,128]{1,0:T(8,128)S(1)}, u32[]{:S(2)}, u32[]{:S(2)}) collective-permute-start(f32[328,128]{1,0:T(8,128)S(1)} %collective-permute-done.29.rest_1_), channel_id=1, source_target_pairs={{0,1},{1,0},{2,3},{3,2},{4,5},{5,4},{6,7},{7,6},{8,9},{9,8},{10,11... | collective-permute-start | bytes 503816 | tf_op jit(solution)/shard_map/ppermute | solution.py:360
  118.8 1.7 %collective-permute-start.34 = (f32[328,128]{1,0:T(8,128)S(1)}, f32[328,128]{1,0:T(8,128)S(1)}, u32[]{:S(2)}, u32[]{:S(2)}) collective-permute-start(f32[328,128]{1,0:T(8,128)S(1)} %collective-permute-done.30.rest_2_), channel_id=1, source_target_pairs={{0,1},{1,0},{2,3},{3,2},{4,5},{5,4},{6,7},{7,6},{8,9},{9,8},{10,11... | collective-permute-start | bytes 503816 | tf_op jit(solution)/shard_map/ppermute | solution.py:360
  120.5 0.9 collective-permute-done.31.rest_3_
  121.4 0.8 collective-permute-start.35
  122.3 1.0 collective-permute-done.35.rest_7_
  123.3 4.4 %lower.1 = f32[8,256,256]{2,1,0:T(8,128)} custom-call(s32[50]{0:T(128)S(1)} %concatenate.3.where, f32[8,256,256]{2,1,0:T(8,128)S(1)} %copy-done.1, f32[2,256,256]{2,1,0:T(8,128)S(1)} %copy-done.2, f32[328,128]{1,0:T(8,128)S(1)} %fusion.13.rest_0_, f32[328,128]{1,0:T(8,128)S(1)} %collective-permute-done.29.rest_1_, ...), custom_call_target="tpu_custom_call" | custom-call | flops 1610612736 | bytes 8388608 | tf_op jit(solution)/shard_map/lower/pallas_call | solution.py:475
  (38 shorter events, 0.8 us)
Async XLA Ops:
  3.1 1.6 %copy-start = (f32[8,256,256]{2,1,0:T(8,128)S(1)}, f32[8,256,256]{2,1,0:T(8,128)}, u32[]{:S(2)}) copy-start(f32[8,256,256]{2,1,0:T(8,128)} %transfer.1) | copy-start | bytes 6291460
  4.7 1.6 %copy-start.4 = (f32[8,256,256]{2,1,0:T(8,128)S(1)}, f32[8,256,256]{2,1,0:T(8,128)}, u32[]{:S(2)}) copy-start(f32[8,256,256]{2,1,0:T(8,128)} %child_basis.1) | copy-start | bytes 6291460
  6.2 13.2 %copy-start.3 = (f32[12,256,256]{2,1,0:T(8,128)S(1)}, f32[12,256,256]{2,1,0:T(8,128)}, u32[]{:S(2)}) copy-start(f32[12,256,256]{2,1,0:T(8,128)} %child_blocks.3) | copy-start | bytes 9437188
  6.2 13.2 %copy-start.5 = (f32[8,256,256]{2,1,0:T(8,128)S(1)}, f32[8,256,256]{2,1,0:T(8,128)}, u32[]{:S(2)}) copy-start(f32[8,256,256]{2,1,0:T(8,128)} %parent_blocks.3) | copy-start | bytes 6291460
  10.3 16.9 %collective-permute-start = (f32[328,128]{1,0:T(8,128)S(1)}, f32[328,128]{1,0:T(8,128)S(1)}, u32[]{:S(2)}, u32[]{:S(2)}) collective-permute-start(f32[328,128]{1,0:T(8,128)S(1)} %get-tuple-element.44), channel_id=1, source_target_pairs={{0,240},{8,248},{16,0},{24,8},{32,16},{40,24},{48,32},{56,40},{64,... | collective-permute-start | bytes 503816 | tf_op jit(solution)/shard_map/ppermute | solution.py:352
  19.4 1.0 copy-start.6
  27.2 18.1 %collective-permute-start.2 = (f32[4,3,328,128]{3,2,1,0:T(8,128)S(1)}, f32[4,3,328,128]{3,2,1,0:T(8,128)S(1)}, u32[]{:S(2)}, u32[]{:S(2)}) collective-permute-start(f32[4,3,328,128]{3,2,1,0:T(8,128)S(1)} %get-tuple-element.51), channel_id=1, source_target_pairs={{0,1},{1,0},{2,3},{3,2},{4,5},{5,4},{6,7},{7,6},{8,9},{9,8},{10,11... | collective-permute-start | bytes 6045704 | tf_op jit(solution)/shard_map/ppermute | solution.py:360
  28.2 6.8 %collective-permute-start.1 = (f32[328,128]{1,0:T(8,128)S(1)}, f32[328,128]{1,0:T(8,128)S(1)}, u32[]{:S(2)}, u32[]{:S(2)}) collective-permute-start(f32[328,128]{1,0:T(8,128)S(1)} %collective-permute-done.rest_0_), channel_id=1, source_target_pairs={{0,248},{8,0},{16,8},{24,16},{32,24},{40,32},{48,40},{56,48},{64,5... | collective-permute-start | bytes 503816 | tf_op jit(solution)/shard_map/ppermute | solution.py:352
  31.2 9.6 %collective-permute-start.3 = (f32[328,128]{1,0:T(8,128)S(1)}, f32[328,128]{1,0:T(8,128)S(1)}, u32[]{:S(2)}, u32[]{:S(2)}) collective-permute-start(f32[328,128]{1,0:T(8,128)S(1)} %collective-permute-done.rest_0_), channel_id=1, source_target_pairs={{0,6},{1,7},{2,0},{3,1},{4,2},{5,3},{6,4},{7,5},{8,14},{9,15},{10,... | collective-permute-start | bytes 503816 | tf_op jit(solution)/shard_map/ppermute | solution.py:356
  34.0 6.9 %collective-permute-start.4 = (f32[328,128]{1,0:T(8,128)S(1)}, f32[328,128]{1,0:T(8,128)S(1)}, u32[]{:S(2)}, u32[]{:S(2)}) collective-permute-start(f32[328,128]{1,0:T(8,128)S(1)} %collective-permute-done.rest_0_), channel_id=1, source_target_pairs={{0,4},{1,5},{2,6},{3,7},{4,0},{5,1},{6,2},{7,3},{8,12},{9,13},{10,... | collective-permute-start | bytes 503816 | tf_op jit(solution)/shard_map/ppermute | solution.py:356
  34.3 11.0 %collective-permute-start.5 = (f32[328,128]{1,0:T(8,128)S(1)}, f32[328,128]{1,0:T(8,128)S(1)}, u32[]{:S(2)}, u32[]{:S(2)}) collective-permute-start(f32[328,128]{1,0:T(8,128)S(1)} %collective-permute-done.rest_0_), channel_id=1, source_target_pairs={{0,2},{1,3},{2,4},{3,5},{4,6},{5,7},{6,0},{7,1},{8,10},{9,11},{10,... | collective-permute-start | bytes 503816 | tf_op jit(solution)/shard_map/ppermute | solution.py:356
  35.0 19.1 %collective-permute-start.6 = (f32[4,328,128]{2,1,0:T(8,128)S(1)}, f32[4,328,128]{2,1,0:T(8,128)S(1)}, u32[]{:S(2)}, u32[]{:S(2)}) collective-permute-start(f32[4,328,128]{2,1,0:T(8,128)S(1)} %get-tuple-element.53.own_same), channel_id=1, source_target_pairs={{0,248},{8,0},{16,8},{24,16},{32,24},{40,32},{48,40},{56,48},{64,5... | collective-permute-start | bytes 2015240 | tf_op jit(solution)/shard_map/ppermute | solution.py:352
  45.4 19.6 %collective-permute-start.7 = (f32[4,328,128]{2,1,0:T(8,128)S(1)}, f32[4,328,128]{2,1,0:T(8,128)S(1)}, u32[]{:S(2)}, u32[]{:S(2)}) collective-permute-start(f32[4,328,128]{2,1,0:T(8,128)S(1)} %add_bitcast_fusion), channel_id=1, source_target_pairs={{0,8},{8,16},{16,24},{24,32},{32,40},{40,48},{48,56},{56,64},{64,7... | collective-permute-start | bytes 2015240 | tf_op jit(solution)/shard_map/ppermute | solution.py:352
  45.6 9.0 %collective-permute-start.10 = (f32[2,328,128]{2,1,0:T(8,128)S(1)}, f32[2,328,128]{2,1,0:T(8,128)S(1)}, u32[]{:S(2)}, u32[]{:S(2)}) collective-permute-start(f32[2,328,128]{2,1,0:T(8,128)S(1)} %get-tuple-element.86), channel_id=1, source_target_pairs={{0,6},{1,7},{2,0},{3,1},{4,2},{5,3},{6,4},{7,5},{8,14},{9,15},{10,... | collective-permute-start | bytes 1007624 | tf_op jit(solution)/shard_map/ppermute | solution.py:356
  45.7 10.3 %collective-permute-start.8 = (f32[2,328,128]{2,1,0:T(8,128)S(1)}, f32[2,328,128]{2,1,0:T(8,128)S(1)}, u32[]{:S(2)}, u32[]{:S(2)}) collective-permute-start(f32[2,328,128]{2,1,0:T(8,128)S(1)} %get-tuple-element.88), channel_id=1, source_target_pairs={{0,2},{1,3},{2,4},{3,5},{4,6},{5,7},{6,0},{7,1},{8,10},{9,11},{10,... | collective-permute-start | bytes 1007624 | tf_op jit(solution)/shard_map/ppermute | solution.py:356
  47.1 14.8 %collective-permute-start.9 = (f32[2,328,128]{2,1,0:T(8,128)S(1)}, f32[2,328,128]{2,1,0:T(8,128)S(1)}, u32[]{:S(2)}, u32[]{:S(2)}) collective-permute-start(f32[2,328,128]{2,1,0:T(8,128)S(1)} %get-tuple-element.87), channel_id=1, source_target_pairs={{0,4},{1,5},{2,6},{3,7},{4,0},{5,1},{6,2},{7,3},{8,12},{9,13},{10,... | collective-permute-start | bytes 1007624 | tf_op jit(solution)/shard_map/ppermute | solution.py:356
  65.0 13.2 %collective-permute-start.15 = (f32[4,328,128]{2,1,0:T(8,128)S(1)}, f32[4,328,128]{2,1,0:T(8,128)S(1)}, u32[]{:S(2)}, u32[]{:S(2)}) collective-permute-start(f32[4,328,128]{2,1,0:T(8,128)S(1)} %collective-permute-done.6.first), channel_id=1, source_target_pairs={{0,1},{1,0},{2,3},{3,2},{4,5},{5,4},{6,7},{7,6},{8,9},{9,8},{10,11... | collective-permute-start | bytes 2015240 | tf_op jit(solution)/shard_map/ppermute | solution.py:360
  66.4 9.5 %collective-permute-start.11 = (f32[328,128]{1,0:T(8,128)S(1)}, f32[328,128]{1,0:T(8,128)S(1)}, u32[]{:S(2)}, u32[]{:S(2)}) collective-permute-start(f32[328,128]{1,0:T(8,128)S(1)} %slice_bitcast_fusion.1), channel_id=1, source_target_pairs={{0,8},{8,16},{16,24},{24,32},{32,40},{40,48},{48,56},{56,64},{64,7... | collective-permute-start | bytes 503816 | tf_op jit(solution)/shard_map/ppermute | solution.py:352
  66.7 9.2 %collective-permute-start.12 = (f32[328,128]{1,0:T(8,128)S(1)}, f32[328,128]{1,0:T(8,128)S(1)}, u32[]{:S(2)}, u32[]{:S(2)}) collective-permute-start(f32[328,128]{1,0:T(8,128)S(1)} %collective-permute-done.1.rest_8_), channel_id=1, source_target_pairs={{0,6},{1,7},{2,0},{3,1},{4,2},{5,3},{6,4},{7,5},{8,14},{9,15},{10,... | collective-permute-start | bytes 503816 | tf_op jit(solution)/shard_map/ppermute | solution.py:356
  66.8 9.1 %collective-permute-start.13 = (f32[328,128]{1,0:T(8,128)S(1)}, f32[328,128]{1,0:T(8,128)S(1)}, u32[]{:S(2)}, u32[]{:S(2)}) collective-permute-start(f32[328,128]{1,0:T(8,128)S(1)} %collective-permute-done.1.rest_8_), channel_id=1, source_target_pairs={{0,4},{1,5},{2,6},{3,7},{4,0},{5,1},{6,2},{7,3},{8,12},{9,13},{10,... | collective-permute-start | bytes 503816 | tf_op jit(solution)/shard_map/ppermute | solution.py:356
  67.2 11.0 %collective-permute-start.14 = (f32[328,128]{1,0:T(8,128)S(1)}, f32[328,128]{1,0:T(8,128)S(1)}, u32[]{:S(2)}, u32[]{:S(2)}) collective-permute-start(f32[328,128]{1,0:T(8,128)S(1)} %collective-permute-done.1.rest_8_), channel_id=1, source_target_pairs={{0,2},{1,3},{2,4},{3,5},{4,6},{5,7},{6,0},{7,1},{8,10},{9,11},{10,... | collective-permute-start | bytes 503816 | tf_op jit(solution)/shard_map/ppermute | solution.py:356
  78.2 1.5 %collective-permute-start.16 = (f32[328,128]{1,0:T(8,128)S(1)}, f32[328,128]{1,0:T(8,128)S(1)}, u32[]{:S(2)}, u32[]{:S(2)}) collective-permute-start(f32[328,128]{1,0:T(8,128)S(1)} %collective-permute-done.rest_0_), channel_id=1, source_target_pairs={{0,1},{1,0},{2,3},{3,2},{4,5},{5,4},{6,7},{7,6},{8,9},{9,8},{10,11... | collective-permute-start | bytes 503816 | tf_op jit(solution)/shard_map/ppermute | solution.py:360
  78.7 1.4 %collective-permute-start.17 = (f32[328,128]{1,0:T(8,128)S(1)}, f32[328,128]{1,0:T(8,128)S(1)}, u32[]{:S(2)}, u32[]{:S(2)}) collective-permute-start(f32[328,128]{1,0:T(8,128)S(1)} %collective-permute-done.3.rest_1_), channel_id=1, source_target_pairs={{0,1},{1,0},{2,3},{3,2},{4,5},{5,4},{6,7},{7,6},{8,9},{9,8},{10,11... | collective-permute-start | bytes 503816 | tf_op jit(solution)/shard_map/ppermute | solution.py:360
  78.7 1.6 %collective-permute-start.18 = (f32[328,128]{1,0:T(8,128)S(1)}, f32[328,128]{1,0:T(8,128)S(1)}, u32[]{:S(2)}, u32[]{:S(2)}) collective-permute-start(f32[328,128]{1,0:T(8,128)S(1)} %collective-permute-done.4.rest_2_), channel_id=1, source_target_pairs={{0,1},{1,0},{2,3},{3,2},{4,5},{5,4},{6,7},{7,6},{8,9},{9,8},{10,11... | collective-permute-start | bytes 503816 | tf_op jit(solution)/shard_map/ppermute | solution.py:360
  79.2 1.4 %collective-permute-start.19 = (f32[328,128]{1,0:T(8,128)S(1)}, f32[328,128]{1,0:T(8,128)S(1)}, u32[]{:S(2)}, u32[]{:S(2)}) collective-permute-start(f32[328,128]{1,0:T(8,128)S(1)} %collective-permute-done.5.rest_3_), channel_id=1, source_target_pairs={{0,1},{1,0},{2,3},{3,2},{4,5},{5,4},{6,7},{7,6},{8,9},{9,8},{10,11... | collective-permute-start | bytes 503816 | tf_op jit(solution)/shard_map/ppermute | solution.py:360
  79.2 1.6 %collective-permute-start.20 = (f32[328,128]{1,0:T(8,128)S(1)}, f32[328,128]{1,0:T(8,128)S(1)}, u32[]{:S(2)}, u32[]{:S(2)}) collective-permute-start(f32[328,128]{1,0:T(8,128)S(1)} %collective-permute-done.1.rest_8_), channel_id=1, source_target_pairs={{0,1},{1,0},{2,3},{3,2},{4,5},{5,4},{6,7},{7,6},{8,9},{9,8},{10,11... | collective-permute-start | bytes 503816 | tf_op jit(solution)/shard_map/ppermute | solution.py:360
  79.7 1.4 %collective-permute-start.21 = (f32[328,128]{1,0:T(8,128)S(1)}, f32[328,128]{1,0:T(8,128)S(1)}, u32[]{:S(2)}, u32[]{:S(2)}) collective-permute-start(f32[328,128]{1,0:T(8,128)S(1)} %collective-permute-done.12.rest_9_), channel_id=1, source_target_pairs={{0,1},{1,0},{2,3},{3,2},{4,5},{5,4},{6,7},{7,6},{8,9},{9,8},{10,11... | collective-permute-start | bytes 503816 | tf_op jit(solution)/shard_map/ppermute | solution.py:360
  80.1 1.4 %collective-permute-start.22 = (f32[328,128]{1,0:T(8,128)S(1)}, f32[328,128]{1,0:T(8,128)S(1)}, u32[]{:S(2)}, u32[]{:S(2)}) collective-permute-start(f32[328,128]{1,0:T(8,128)S(1)} %collective-permute-done.13.rest_10_), channel_id=1, source_target_pairs={{0,1},{1,0},{2,3},{3,2},{4,5},{5,4},{6,7},{7,6},{8,9},{9,8},{10,11... | collective-permute-start | bytes 503816 | tf_op jit(solution)/shard_map/ppermute | solution.py:360
  80.3 1.4 %collective-permute-start.23 = (f32[328,128]{1,0:T(8,128)S(1)}, f32[328,128]{1,0:T(8,128)S(1)}, u32[]{:S(2)}, u32[]{:S(2)}) collective-permute-start(f32[328,128]{1,0:T(8,128)S(1)} %collective-permute-done.14.rest_11_), channel_id=1, source_target_pairs={{0,1},{1,0},{2,3},{3,2},{4,5},{5,4},{6,7},{7,6},{8,9},{9,8},{10,11... | collective-permute-start | bytes 503816 | tf_op jit(solution)/shard_map/ppermute | solution.py:360
  80.6 13.6 %collective-permute-start.24 = (f32[328,128]{1,0:T(8,128)S(1)}, f32[328,128]{1,0:T(8,128)S(1)}, u32[]{:S(2)}, u32[]{:S(2)}) collective-permute-start(f32[328,128]{1,0:T(8,128)S(1)} %fusion.14), channel_id=1, source_target_pairs={{0,16},{8,24},{16,32},{24,40},{32,48},{40,56},{48,64},{56,72},{64,... | collective-permute-start | bytes 503816 | tf_op jit(solution)/shard_map/ppermute | solution.py:352
  89.3 34.0 %copy-start.1 = (f32[8,256,256]{2,1,0:T(8,128)S(1)}, f32[8,256,256]{2,1,0:T(8,128)}, u32[]{:S(2)}) copy-start(f32[8,256,256]{2,1,0:T(8,128)} %transfer.1) | copy-start | bytes 6291460
  89.3 34.0 %copy-start.2 = (f32[2,256,256]{2,1,0:T(8,128)S(1)}, f32[2,256,256]{2,1,0:T(8,128)}, u32[]{:S(2)}) copy-start(f32[2,256,256]{2,1,0:T(8,128)} %upper.1) | copy-start | bytes 1572868
  94.2 2.8 %collective-permute-start.25 = (f32[4,328,128]{2,1,0:T(8,128)S(1)}, f32[4,328,128]{2,1,0:T(8,128)S(1)}, u32[]{:S(2)}, u32[]{:S(2)}) collective-permute-start(f32[4,328,128]{2,1,0:T(8,128)S(1)} %get-tuple-element.84), channel_id=1, source_target_pairs={{0,1},{1,0},{2,3},{3,2},{4,5},{5,4},{6,7},{7,6},{8,9},{9,8},{10,11... | collective-permute-start | bytes 2015240 | tf_op jit(solution)/shard_map/ppermute | solution.py:360
  97.1 7.5 %collective-permute-start.26 = (f32[328,128]{1,0:T(8,128)S(1)}, f32[328,128]{1,0:T(8,128)S(1)}, u32[]{:S(2)}, u32[]{:S(2)}) collective-permute-start(f32[328,128]{1,0:T(8,128)S(1)} %get-tuple-element.89), channel_id=1, source_target_pairs={{0,2},{1,3},{2,4},{3,5},{4,6},{5,7},{6,0},{7,1},{8,10},{9,11},{10,... | collective-permute-start | bytes 503816 | tf_op jit(solution)/shard_map/ppermute | solution.py:356
  97.2 9.7 %collective-permute-start.27 = (f32[328,128]{1,0:T(8,128)S(1)}, f32[328,128]{1,0:T(8,128)S(1)}, u32[]{:S(2)}, u32[]{:S(2)}) collective-permute-start(f32[328,128]{1,0:T(8,128)S(1)} %get-tuple-element.91), channel_id=1, source_target_pairs={{0,4},{1,5},{2,6},{3,7},{4,0},{5,1},{6,2},{7,3},{8,12},{9,13},{10,... | collective-permute-start | bytes 503816 | tf_op jit(solution)/shard_map/ppermute | solution.py:356
  99.2 8.7 %collective-permute-start.28 = (f32[328,128]{1,0:T(8,128)S(1)}, f32[328,128]{1,0:T(8,128)S(1)}, u32[]{:S(2)}, u32[]{:S(2)}) collective-permute-start(f32[328,128]{1,0:T(8,128)S(1)} %get-tuple-element.90), channel_id=1, source_target_pairs={{0,6},{1,7},{2,0},{3,1},{4,2},{5,3},{6,4},{7,5},{8,14},{9,15},{10,... | collective-permute-start | bytes 503816 | tf_op jit(solution)/shard_map/ppermute | solution.py:356
  107.9 9.5 %collective-permute-start.29 = (f32[328,128]{1,0:T(8,128)S(1)}, f32[328,128]{1,0:T(8,128)S(1)}, u32[]{:S(2)}, u32[]{:S(2)}) collective-permute-start(f32[328,128]{1,0:T(8,128)S(1)} %fusion.13.rest_0_), channel_id=1, source_target_pairs={{0,6},{1,7},{2,0},{3,1},{4,2},{5,3},{6,4},{7,5},{8,14},{9,15},{10,... | collective-permute-start | bytes 503816 | tf_op jit(solution)/shard_map/ppermute | solution.py:356
  110.7 8.1 %collective-permute-start.30 = (f32[328,128]{1,0:T(8,128)S(1)}, f32[328,128]{1,0:T(8,128)S(1)}, u32[]{:S(2)}, u32[]{:S(2)}) collective-permute-start(f32[328,128]{1,0:T(8,128)S(1)} %fusion.13.rest_0_), channel_id=1, source_target_pairs={{0,4},{1,5},{2,6},{3,7},{4,0},{5,1},{6,2},{7,3},{8,12},{9,13},{10,... | collective-permute-start | bytes 503816 | tf_op jit(solution)/shard_map/ppermute | solution.py:356
  110.7 10.7 %collective-permute-start.31 = (f32[328,128]{1,0:T(8,128)S(1)}, f32[328,128]{1,0:T(8,128)S(1)}, u32[]{:S(2)}, u32[]{:S(2)}) collective-permute-start(f32[328,128]{1,0:T(8,128)S(1)} %fusion.13.rest_0_), channel_id=1, source_target_pairs={{0,2},{1,3},{2,4},{3,5},{4,6},{5,7},{6,0},{7,1},{8,10},{9,11},{10,... | collective-permute-start | bytes 503816 | tf_op jit(solution)/shard_map/ppermute | solution.py:356
  111.4 10.8 %collective-permute-start.32 = (f32[328,128]{1,0:T(8,128)S(1)}, f32[328,128]{1,0:T(8,128)S(1)}, u32[]{:S(2)}, u32[]{:S(2)}) collective-permute-start(f32[328,128]{1,0:T(8,128)S(1)} %fusion.13.rest_0_), channel_id=1, source_target_pairs={{0,1},{1,0},{2,3},{3,2},{4,5},{5,4},{6,7},{7,6},{8,9},{9,8},{10,11... | collective-permute-start | bytes 503816 | tf_op jit(solution)/shard_map/ppermute | solution.py:360
  117.4 4.8 %collective-permute-start.33 = (f32[328,128]{1,0:T(8,128)S(1)}, f32[328,128]{1,0:T(8,128)S(1)}, u32[]{:S(2)}, u32[]{:S(2)}) collective-permute-start(f32[328,128]{1,0:T(8,128)S(1)} %collective-permute-done.29.rest_1_), channel_id=1, source_target_pairs={{0,1},{1,0},{2,3},{3,2},{4,5},{5,4},{6,7},{7,6},{8,9},{9,8},{10,11... | collective-permute-start | bytes 503816 | tf_op jit(solution)/shard_map/ppermute | solution.py:360
  118.8 3.4 %collective-permute-start.34 = (f32[328,128]{1,0:T(8,128)S(1)}, f32[328,128]{1,0:T(8,128)S(1)}, u32[]{:S(2)}, u32[]{:S(2)}) collective-permute-start(f32[328,128]{1,0:T(8,128)S(1)} %collective-permute-done.30.rest_2_), channel_id=1, source_target_pairs={{0,1},{1,0},{2,3},{3,2},{4,5},{5,4},{6,7},{7,6},{8,9},{9,8},{10,11... | collective-permute-start | bytes 503816 | tf_op jit(solution)/shard_map/ppermute | solution.py:360
  121.4 1.9 %collective-permute-start.35 = (f32[328,128]{1,0:T(8,128)S(1)}, f32[328,128]{1,0:T(8,128)S(1)}, u32[]{:S(2)}, u32[]{:S(2)}) collective-permute-start(f32[328,128]{1,0:T(8,128)S(1)} %collective-permute-done.31.rest_3_), channel_id=1, source_target_pairs={{0,1},{1,0},{2,3},{3,2},{4,5},{5,4},{6,7},{7,6},{8,9},{9,8},{10,11... | collective-permute-start | bytes 503816 | tf_op jit(solution)/shard_map/ppermute | solution.py:360
where the time goes:
time: 128 us
  waiting for transfers between devices  54.4 us (42%)
  starting transfers between devices  42.6 us (33%)
  Pallas kernels  22.7 us (18%)
  local copies, waits for them, and re-layouts  6.68 us (5%)
    ppermute x15, waiting for transfers between devices, to_y(): lax.ppermute(value, 'pair', [(i, (i + 2 * steps) % PAIR) for i in range(P...  28.4 us
    ppermute x6, waiting for transfers between devices, to_clus(): lax.ppermute(value, 'clus', [(i, (i + steps) % count) for i in range(coun...  22.2 us
    ppermute x6, starting transfers between devices, to_clus(): lax.ppermute(value, 'clus', [(i, (i + steps) % count) for i in range(coun...  18 us
    ppermute x15, starting transfers between devices, to_y(): lax.ppermute(value, 'pair', [(i, (i + 2 * steps) % PAIR) for i in range(P...  13.4 us
    ppermute x15, starting transfers between devices, to_core(): return lax.ppermute(value, 'pair', [(i, i ^ 1) for i in range(PAIR)])  11.1 us
    pallas_call x1, Pallas kernels, per_device(): call(near_kernel, 'near', (floats(4, SHARE, HALF), floats(4, SHARE, HALF)...  7.55 us
    pallas_call x1, Pallas kernels, per_device(): call(far_kernel, 'far', (floats(4, REACH, SHARE, HALF), floats(4, REACH,...  6.67 us
    unnamed x16, local copies, waits for them, and re-layouts  5.77 us
  transfers between devices with their start and end apart: 36, of which 21 were waited for; matrix products, arithmetic and copies ran while one was open for 0% of the time, Pallas kernels for 11%

commit v1 on v0

--- a/solution.py
+++ b/solution.py
@@ -209,21 +209,24 @@
 
 
 def near_kernel(
-    where, after, also_after, child_blocks, parent_blocks, own_terms, own_same, own_other, first, other_first,
-    *rest,
+    where, after, also_after, child_blocks, parent_blocks, own_terms, own_same, own_other,
+    mine, other, *rest,
 ):
-    pieces = rest[: 2 * PAIR]
-    kept, sent, window, total, rows_of_parents = rest[2 * PAIR :]
+    pieces = rest[:PAIR]
+    kept, sent, window, total, rows_of_parents = rest[PAIR:]
     clus, me = where[0], where[1]
-    halves = ((own_same, 0, 0), (own_other, 4, 0), (first, 0, 1), (other_first, 4, 1))
-    for source, first_place, offset in halves:
+    halves = (
+        (own_same, 0, 0, 0), (own_other, 0, 4, 0),
+        (mine, 0, 0, 1), (other, 0, 4, 1), (mine, 4, 0, 2), (other, 4, 4, 2),
+    )
+    for source, start, first_place, offset in halves:
 
         def take_half(at):
-            window[first_place + at, offset] = source[at]
+            window[first_place + at, offset] = source[start + at]
 
         each(4, take_half)
-    for i, piece in enumerate(pieces):
-        window[i % PAIR, 2 + i // PAIR] = piece[...]
+    for place, piece in enumerate(pieces):
+        window[place, REACH] = piece[...]
     child_groups = child_blocks.shape[0] // UNROLL
     parent_groups = parent_blocks.shape[0] // UNROLL
     cleared(total)
@@ -425,34 +428,33 @@
 
     second, own_same, kept, sent = lax.optimization_barrier((second, own_same, kept, sent))
     barrier = lax.optimization_barrier
-    third = to_clus(second, -1)
+    chain = to_clus(jnp.concatenate([own_same, second[None]]), -1)
     got = to_core(sent)
-    seconds = [second] + [to_y(second, -step) for step in range(1, 4)]
-    third, got, seconds = barrier((third, got, seconds))
-
-    first = to_clus(own_same, -1)
     far_first = to_clus(kept[:, 0] + got[:, 0], 1)
     parts = [kept[step, 1:] + got[step, 1:] for step in range(4)]
-    received = [to_y(parts[step], step) for step in range(1, 4)]
-    first, far_first, received, third, seconds = barrier(
-        (first, far_first, received, third, seconds)
-    )
-
-    far_sum = parts[0] + received[0] + received[1] + received[2]
+    received = [
+        to_y(jnp.concatenate([parts[step], second[None]]), step) for step in range(1, 4)
+    ]
+    chain, far_first, received = barrier((chain, far_first, received))
+
+    far_sum = parts[0] + received[0][:2] + received[1][:2] + received[2][:2]
     far_third = to_clus(far_sum[1], 1)
+    third = chain[4]
     thirds = [third] + [to_y(third, -step) for step in range(1, 4)]
-    other_first = to_core(first)
-    far_third, thirds, other_first, seconds = barrier((far_third, thirds, other_first, seconds))
+    mine = jnp.concatenate(
+        [chain[:4], second[None], received[2][2:], received[1][2:], received[0][2:]]
+    )
+    other = to_core(mine)
+    far_third, thirds, other, mine = barrier((far_third, thirds, other, mine))
 
     far_later = to_clus(far_sum[0] + far_third, 2)
-    second_pieces = seconds + [to_core(piece) for piece in seconds]
     third_pieces = thirds + [to_core(piece) for piece in thirds]
 
     kept, sent = call(
         near_kernel,
         "near",
         (floats(4, SHARE, HALF), floats(4, SHARE, HALF)),
-        [SMEM, ANY, ANY, VMEM, VMEM, VMEM] + [VMEM] * (2 * PAIR + 4),
+        [SMEM, ANY, ANY, VMEM, VMEM, VMEM] + [VMEM] * (PAIR + 4),
         (VMEM, VMEM),
         [
             pltpu.VMEM((PAIR, REACH + 1, SHARE, HALF), jnp.float32),
@@ -462,7 +464,7 @@
         40,
     )(
         where, far_third, far_first, child_blocks, parent_blocks, own_terms, own_same, own_other,
-        first, other_first, *second_pieces, *third_pieces,
+        mine, other, *third_pieces,
     )
 
     kept, sent, far_later = lax.optimization_barrier((kept, sent, far_later))

time: 128 us -> 119 us (0.930)
  waiting for transfers between devices: 54.4 us -> 46.2 us
    ppermute x15 -> x12, waiting for transfers between devices: 28.4 us -> 22 us  [to_y(): lax.ppermute(value, 'pair', [(i, (i + 2 * steps) % PAIR) for i in range(P...]
    ppermute x6 -> x5, starting transfers between devices: 18 us -> 14.1 us  [to_clus(): lax.ppermute(value, 'clus', [(i, (i + steps) % count) for i in range(coun...]
    ppermute x15 -> x11, starting transfers between devices: 11.1 us -> 14.8 us  [to_core(): return lax.ppermute(value, 'pair', [(i, i ^ 1) for i in range(PAIR)])]
    ppermute x6 -> x5, waiting for transfers between devices: 22.2 us -> 20.5 us  [to_clus(): lax.ppermute(value, 'clus', [(i, (i + steps) % count) for i in range(coun...]
    ppermute x15 -> x12, starting transfers between devices: 13.4 us -> 13 us  [to_y(): lax.ppermute(value, 'pair', [(i, (i + 2 * steps) % PAIR) for i in range(P...]
    unnamed x16 -> x20, local copies, waits for them, and re-layouts: 5.77 us -> 5.85 us
    ppermute x15 -> x11, waiting for transfers between devices: 3.8 us -> 3.78 us  [to_core(): return lax.ppermute(value, 'pair', [(i, i ^ 1) for i in range(PAIR)])]
  transfers between devices with their start and end apart: 36 -> 28, of which waited for: 21 -> 15; matrix products, arithmetic and copies ran while one was open for 0% -> 0% of each run, Pallas kernels for 11% -> 12%
where the time goes in v1:
time: 119 us
  waiting for transfers between devices  46.2 us (39%)
  starting transfers between devices  41.9 us (35%)
  Pallas kernels  22.6 us (19%)
  local copies, waits for them, and re-layouts  6.79 us (6%)
    ppermute x12, waiting for transfers between devices, to_y(): lax.ppermute(value, 'pair', [(i, (i + 2 * steps) % PAIR) for i in range(P...  22 us
    ppermute x5, waiting for transfers between devices, to_clus(): lax.ppermute(value, 'clus', [(i, (i + steps) % count) for i in range(coun...  20.5 us
    ppermute x11, starting transfers between devices, to_core(): return lax.ppermute(value, 'pair', [(i, i ^ 1) for i in range(PAIR)])  14.8 us
    ppermute x5, starting transfers between devices, to_clus(): lax.ppermute(value, 'clus', [(i, (i + steps) % count) for i in range(coun...  14.1 us
    ppermute x12, starting transfers between devices, to_y(): lax.ppermute(value, 'pair', [(i, (i + 2 * steps) % PAIR) for i in range(P...  13 us
    pallas_call x1, Pallas kernels, per_device(): call(near_kernel, 'near', (floats(4, SHARE, HALF), floats(4, SHARE, HALF)...  7.54 us
    pallas_call x1, Pallas kernels, per_device(): call(far_kernel, 'far', (floats(4, REACH, SHARE, HALF), floats(4, REACH,...  6.67 us
    unnamed x20, local copies, waits for them, and re-layouts  5.85 us
  transfers between devices with their start and end apart: 28, of which 15 were waited for; matrix products, arithmetic and copies ran while one was open for 0% of the time, Pallas kernels for 12%

profile of v1, /device:TPU:1, one launch (start us, length us, event | category | flops | bytes accessed | tf_op | source)
XLA Modules:
  0.0 118.9 jit_solution(5517986104805620723)
XLA Ops:
  0.6 0.8 copy.13
  1.4 0.1 reshape.28
  1.5 0.8 copy.12
  2.2 0.1 reshape.27
  2.3 0.7 concatenate.18.where
  3.1 1.6 %copy-done = f32[8,256,256]{2,1,0:T(8,128)S(1)} copy-done((f32[8,256,256]{2,1,0:T(8,128)S(1)}, f32[8,256,256]{2,1,0:T(8,128)}, u32[]{:S(2)}) %copy-start) | copy-done | bytes 2097176
  4.7 1.6 %copy-done.4 = f32[8,256,256]{2,1,0:T(8,128)S(1)} copy-done((f32[8,256,256]{2,1,0:T(8,128)S(1)}, f32[8,256,256]{2,1,0:T(8,128)}, u32[]{:S(2)}) %copy-start.4) | copy-done | bytes 2097176
  6.3 4.0 %lift.1 = (f32[2,256,256]{2,1,0:T(8,128)}, f32[4,328,128]{2,1,0:T(8,128)S(1)}, f32[4,328,128]{2,1,0:T(8,128)S(1)}, f32[328,128]{1,0:T(8,128)S(1)}) custom-call(s32[50]{0:T(128)S(1)} %concatenate.18.where, f32[8,256,256]{2,1,0:T(8,128)S(1)} %copy-done.4, f32[8,256,256]{2,1,0:T(8,128)S(1)} %copy-done), custom_call_target="tpu_custom_call" | custom-call | flops 1610612736 | bytes 8388608 | tf_op jit(solution)/shard_map/lift/pallas_call | solution.py:391
  10.3 9.1 %collective-permute-start = (f32[328,128]{1,0:T(8,128)S(1)}, f32[328,128]{1,0:T(8,128)S(1)}, u32[]{:S(2)}, u32[]{:S(2)}) collective-permute-start(f32[328,128]{1,0:T(8,128)S(1)} %get-tuple-element.30), channel_id=1, source_target_pairs={{0,240},{8,248},{16,0},{24,8},{32,16},{40,24},{48,32},{56,40},{64,... | collective-permute-start | bytes 503816 | tf_op jit(solution)/shard_map/ppermute | solution.py:355
  19.4 1.0 copy-done.6
  20.5 6.7 %far.1 = (f32[4,3,328,128]{3,2,1,0:T(8,128)S(1)}, f32[4,3,328,128]{3,2,1,0:T(8,128)S(1)}, f32[8,328,128]{2,1,0:T(8,128)S(1)}) custom-call(s32[50]{0:T(128)S(1)} %concatenate.18.where, f32[8,256,256]{2,1,0:T(8,128)S(1)} %copy-done.4, f32[2,256,256]{2,1,0:T(8,128)S(1)} %copy-done.6, f32[12,256,256]{2,1,0:T(8,128)S(1)} %copy-done.3, f32[8,256,256]{2,1,0:T(8,128)S(1)} %copy-done.5), custom_call_target="tpu_custom_call" | custom-call | flops 4026531840 | bytes 8388608 | tf_op jit(solution)/shard_map/far/pallas_call | solution.py:413
  27.2 1.0 collective-permute-start.1
  28.2 0.1 pad_maximum_fusion
  28.2 3.1 %collective-permute-start.2 = (f32[5,328,128]{2,1,0:T(8,128)S(1)}, f32[5,328,128]{2,1,0:T(8,128)S(1)}, u32[]{:S(2)}, u32[]{:S(2)}) collective-permute-start(f32[5,328,128]{2,1,0:T(8,128)S(1)} %pad_maximum_fusion), channel_id=1, source_target_pairs={{0,248},{8,0},{16,8},{24,16},{32,24},{40,32},{48,40},{56,48},{64,5... | collective-permute-start | bytes 2519048 | tf_op jit(solution)/shard_map/ppermute | solution.py:355
  31.4 0.5 collective-permute-done.1
  31.9 0.1 fusion
  31.9 0.8 collective-permute-start.3
  32.7 0.1 fusion.1
  32.8 0.1 pad_maximum_fusion.1
  33.0 2.8 %collective-permute-start.6 = (f32[3,328,128]{2,1,0:T(8,128)S(1)}, f32[3,328,128]{2,1,0:T(8,128)S(1)}, u32[]{:S(2)}, u32[]{:S(2)}) collective-permute-start(f32[3,328,128]{2,1,0:T(8,128)S(1)} %get-tuple-element.64), channel_id=1, source_target_pairs={{0,6},{1,7},{2,0},{3,1},{4,2},{5,3},{6,4},{7,5},{8,14},{9,15},{10,... | collective-permute-start | bytes 1511432 | tf_op jit(solution)/shard_map/ppermute | solution.py:359
  35.8 0.3 collective-permute-start.5
  36.1 0.7 collective-permute-start.4
  36.8 12.7 %collective-permute-done.2 = f32[5,328,128]{2,1,0:T(8,128)S(1)} collective-permute-done((f32[5,328,128]{2,1,0:T(8,128)S(1)}, f32[5,328,128]{2,1,0:T(8,128)S(1)}, u32[]{:S(2)}, u32[]{:S(2)}) %collective-permute-start.2) | collective-permute-done | bytes 839712 | tf_op jit(solution)/shard_map/ppermute | solution.py:355
  49.5 12.0 %collective-permute-done.4 = f32[3,328,128]{2,1,0:T(8,128)S(1)} collective-permute-done((f32[3,328,128]{2,1,0:T(8,128)S(1)}, f32[3,328,128]{2,1,0:T(8,128)S(1)}, u32[]{:S(2)}, u32[]{:S(2)}) %collective-permute-start.4) | collective-permute-done | bytes 503840 | tf_op jit(solution)/shard_map/ppermute | solution.py:359
  61.6 0.6 collective-permute-start.11
  62.2 0.1 fusion.7
  62.3 0.1 collective-permute-start.7
  62.4 0.1 collective-permute-start.10
  62.5 1.5 %collective-permute-start.9 = (f32[328,128]{1,0:T(8,128)S(1)}, f32[328,128]{1,0:T(8,128)S(1)}, u32[]{:S(2)}, u32[]{:S(2)}) collective-permute-start(f32[328,128]{1,0:T(8,128)S(1)} %slice_bitcast_fusion.2.rest_0_), channel_id=1, source_target_pairs={{0,4},{1,5},{2,6},{3,7},{4,0},{5,1},{6,2},{7,3},{8,12},{9,13},{10,... | collective-permute-start | bytes 503816 | tf_op jit(solution)/shard_map/ppermute | solution.py:359
  64.0 1.2 collective-permute-start.8
  65.2 6.4 %collective-permute-done.7.after = f32[328,128]{1,0:T(8,128)S(1)} collective-permute-done((f32[328,128]{1,0:T(8,128)S(1)}, f32[328,128]{1,0:T(8,128)S(1)}, u32[]{:S(2)}, u32[]{:S(2)}) %collective-permute-start.7) | collective-permute-done | bytes 167968 | tf_op jit(solution)/shard_map/ppermute | solution.py:355
  71.6 1.3 %collective-permute-done.10.rest_3_ = f32[328,128]{1,0:T(8,128)S(1)} collective-permute-done((f32[328,128]{1,0:T(8,128)S(1)}, f32[328,128]{1,0:T(8,128)S(1)}, u32[]{:S(2)}, u32[]{:S(2)}) %collective-permute-start.10) | collective-permute-done | bytes 167968 | tf_op jit(solution)/shard_map/ppermute | solution.py:359
  73.0 0.0 collective-permute-done.9.rest_2_
  73.0 0.3 collective-permute-done.8.rest_1_
  73.3 1.4 %collective-permute-start.12 = (f32[328,128]{1,0:T(8,128)S(1)}, f32[328,128]{1,0:T(8,128)S(1)}, u32[]{:S(2)}, u32[]{:S(2)}) collective-permute-start(f32[328,128]{1,0:T(8,128)S(1)} %slice_bitcast_fusion.2.rest_0_), channel_id=1, source_target_pairs={{0,1},{1,0},{2,3},{3,2},{4,5},{5,4},{6,7},{7,6},{8,9},{9,8},{10,11... | collective-permute-start | bytes 503816 | tf_op jit(solution)/shard_map/ppermute | solution.py:363
  74.6 0.0 collective-permute-start.13
  74.7 0.5 collective-permute-start.14
  75.2 0.0 collective-permute-start.15
  75.2 0.9 collective-permute-start.16
  76.1 0.2 collective-permute-done.14.rest_6_
  76.3 0.3 collective-permute-done.15.rest_7_
  76.6 7.5 %near.1 = (f32[4,328,128]{2,1,0:T(8,128)S(1)}, f32[4,328,128]{2,1,0:T(8,128)S(1)}) custom-call(s32[50]{0:T(128)S(1)} %concatenate.18.where, f32[328,128]{1,0:T(8,128)S(1)} %collective-permute-done.7.after, f32[4,328,128]{2,1,0:T(8,128)S(1)} %collective-permute-done.3.also_after, f32[12,256,256]{2,1,0:T(8,128)S(1)} %copy-done.3, ...), custom_call_target="tpu_custom_call" | custom-call | flops 4026531840 | bytes 8388608 | tf_op jit(solution)/shard_map/near/pallas_call | solution.py:453
  84.1 1.4 %collective-permute-done.16 = f32[328,128]{1,0:T(8,128)S(1)} collective-permute-done((f32[328,128]{1,0:T(8,128)S(1)}, f32[328,128]{1,0:T(8,128)S(1)}, u32[]{:S(2)}, u32[]{:S(2)}) %collective-permute-start.16) | collective-permute-done | bytes 167968 | tf_op jit(solution)/shard_map/ppermute | solution.py:355
  85.5 2.9 %collective-permute-start.17 = (f32[4,328,128]{2,1,0:T(8,128)S(1)}, f32[4,328,128]{2,1,0:T(8,128)S(1)}, u32[]{:S(2)}, u32[]{:S(2)}) collective-permute-start(f32[4,328,128]{2,1,0:T(8,128)S(1)} %get-tuple-element.56), channel_id=1, source_target_pairs={{0,1},{1,0},{2,3},{3,2},{4,5},{5,4},{6,7},{7,6},{8,9},{9,8},{10,11... | collective-permute-start | bytes 2015240 | tf_op jit(solution)/shard_map/ppermute | solution.py:363
  88.4 1.7 %collective-permute-done.17 = f32[4,328,128]{2,1,0:T(8,128)S(1)} collective-permute-done((f32[4,328,128]{2,1,0:T(8,128)S(1)}, f32[4,328,128]{2,1,0:T(8,128)S(1)}, u32[]{:S(2)}, u32[]{:S(2)}) %collective-permute-start.17) | collective-permute-done | bytes 671776 | tf_op jit(solution)/shard_map/ppermute | solution.py:363
  90.1 0.1 fusion.13
  90.2 0.1 collective-permute-start.18
  90.3 2.7 %collective-permute-start.20 = (f32[328,128]{1,0:T(8,128)S(1)}, f32[328,128]{1,0:T(8,128)S(1)}, u32[]{:S(2)}, u32[]{:S(2)}) collective-permute-start(f32[328,128]{1,0:T(8,128)S(1)} %get-tuple-element.62), channel_id=1, source_target_pairs={{0,6},{1,7},{2,0},{3,1},{4,2},{5,3},{6,4},{7,5},{8,14},{9,15},{10,... | collective-permute-start | bytes 503816 | tf_op jit(solution)/shard_map/ppermute | solution.py:359
  93.0 0.6 collective-permute-start.19
  93.5 3.5 %collective-permute-done.18 = f32[328,128]{1,0:T(8,128)S(1)} collective-permute-done((f32[328,128]{1,0:T(8,128)S(1)}, f32[328,128]{1,0:T(8,128)S(1)}, u32[]{:S(2)}, u32[]{:S(2)}) %collective-permute-start.18) | collective-permute-done | bytes 167968 | tf_op jit(solution)/shard_map/ppermute | solution.py:359
  97.0 0.0 collective-permute-done.20
  97.0 4.2 %collective-permute-done.19 = f32[328,128]{1,0:T(8,128)S(1)} collective-permute-done((f32[328,128]{1,0:T(8,128)S(1)}, f32[328,128]{1,0:T(8,128)S(1)}, u32[]{:S(2)}, u32[]{:S(2)}) %collective-permute-start.19) | collective-permute-done | bytes 167968 | tf_op jit(solution)/shard_map/ppermute | solution.py:359
  101.2 0.1 fusion.19.rest_0_
  101.2 0.6 collective-permute-start.23
  101.9 2.4 %collective-permute-start.22 = (f32[328,128]{1,0:T(8,128)S(1)}, f32[328,128]{1,0:T(8,128)S(1)}, u32[]{:S(2)}, u32[]{:S(2)}) collective-permute-start(f32[328,128]{1,0:T(8,128)S(1)} %fusion.19.rest_0_), channel_id=1, source_target_pairs={{0,4},{1,5},{2,6},{3,7},{4,0},{5,1},{6,2},{7,3},{8,12},{9,13},{10,... | collective-permute-start | bytes 503816 | tf_op jit(solution)/shard_map/ppermute | solution.py:359
  104.3 0.1 collective-permute-start.21
  104.3 2.1 %collective-permute-start.24 = (f32[328,128]{1,0:T(8,128)S(1)}, f32[328,128]{1,0:T(8,128)S(1)}, u32[]{:S(2)}, u32[]{:S(2)}) collective-permute-start(f32[328,128]{1,0:T(8,128)S(1)} %fusion.19.rest_0_), channel_id=1, source_target_pairs={{0,1},{1,0},{2,3},{3,2},{4,5},{5,4},{6,7},{7,6},{8,9},{9,8},{10,11... | collective-permute-start | bytes 503816 | tf_op jit(solution)/shard_map/ppermute | solution.py:363
  106.4 0.7 collective-permute-done.23.rest_3_
  107.1 3.9 %collective-permute-start.27 = (f32[328,128]{1,0:T(8,128)S(1)}, f32[328,128]{1,0:T(8,128)S(1)}, u32[]{:S(2)}, u32[]{:S(2)}) collective-permute-start(f32[328,128]{1,0:T(8,128)S(1)} %collective-permute-done.23.rest_3_), channel_id=1, source_target_pairs={{0,1},{1,0},{2,3},{3,2},{4,5},{5,4},{6,7},{7,6},{8,9},{9,8},{10,11... | collective-permute-start | bytes 503816 | tf_op jit(solution)/shard_map/ppermute | solution.py:363
  111.0 2.1 %collective-permute-start.26 = (f32[328,128]{1,0:T(8,128)S(1)}, f32[328,128]{1,0:T(8,128)S(1)}, u32[]{:S(2)}, u32[]{:S(2)}) collective-permute-start(f32[328,128]{1,0:T(8,128)S(1)} %collective-permute-done.22.rest_2_), channel_id=1, source_target_pairs={{0,1},{1,0},{2,3},{3,2},{4,5},{5,4},{6,7},{7,6},{8,9},{9,8},{10,11... | collective-permute-start | bytes 503816 | tf_op jit(solution)/shard_map/ppermute | solution.py:363
  113.1 0.3 collective-permute-start.25
  113.4 0.7 collective-permute-done.26.rest_6_
  114.2 0.4 collective-permute-done.25.rest_5_
  114.5 4.4 %lower.1 = f32[8,256,256]{2,1,0:T(8,128)} custom-call(s32[50]{0:T(128)S(1)} %concatenate.18.where, f32[8,256,256]{2,1,0:T(8,128)S(1)} %copy-done.1, f32[2,256,256]{2,1,0:T(8,128)S(1)} %copy-done.2, f32[328,128]{1,0:T(8,128)S(1)} %fusion.19.rest_0_, f32[328,128]{1,0:T(8,128)S(1)} %collective-permute-done.21.rest_1_, ...), custom_call_target="tpu_custom_call" | custom-call | flops 1610612736 | bytes 8388608 | tf_op jit(solution)/shard_map/lower/pallas_call | solution.py:477
  (30 shorter events, 0.2 us)
Async XLA Ops:
  3.1 1.6 %copy-start = (f32[8,256,256]{2,1,0:T(8,128)S(1)}, f32[8,256,256]{2,1,0:T(8,128)}, u32[]{:S(2)}) copy-start(f32[8,256,256]{2,1,0:T(8,128)} %transfer.1) | copy-start | bytes 6291460
  4.7 1.6 %copy-start.4 = (f32[8,256,256]{2,1,0:T(8,128)S(1)}, f32[8,256,256]{2,1,0:T(8,128)}, u32[]{:S(2)}) copy-start(f32[8,256,256]{2,1,0:T(8,128)} %child_basis.1) | copy-start | bytes 6291460
  6.2 13.2 %copy-start.3 = (f32[12,256,256]{2,1,0:T(8,128)S(1)}, f32[12,256,256]{2,1,0:T(8,128)}, u32[]{:S(2)}) copy-start(f32[12,256,256]{2,1,0:T(8,128)} %child_blocks.3) | copy-start | bytes 9437188
  6.2 13.2 %copy-start.5 = (f32[8,256,256]{2,1,0:T(8,128)S(1)}, f32[8,256,256]{2,1,0:T(8,128)}, u32[]{:S(2)}) copy-start(f32[8,256,256]{2,1,0:T(8,128)} %parent_blocks.3) | copy-start | bytes 6291460
  10.3 16.8 %collective-permute-start = (f32[328,128]{1,0:T(8,128)S(1)}, f32[328,128]{1,0:T(8,128)S(1)}, u32[]{:S(2)}, u32[]{:S(2)}) collective-permute-start(f32[328,128]{1,0:T(8,128)S(1)} %get-tuple-element.30), channel_id=1, source_target_pairs={{0,240},{8,248},{16,0},{24,8},{32,16},{40,24},{48,32},{56,40},{64,... | collective-permute-start | bytes 503816 | tf_op jit(solution)/shard_map/ppermute | solution.py:355
  19.4 1.0 copy-start.6
  27.2 4.7 %collective-permute-start.1 = (f32[4,3,328,128]{3,2,1,0:T(8,128)S(1)}, f32[4,3,328,128]{3,2,1,0:T(8,128)S(1)}, u32[]{:S(2)}, u32[]{:S(2)}) collective-permute-start(f32[4,3,328,128]{3,2,1,0:T(8,128)S(1)} %get-tuple-element.36), channel_id=1, source_target_pairs={{0,1},{1,0},{2,3},{3,2},{4,5},{5,4},{6,7},{7,6},{8,9},{9,8},{10,11... | collective-permute-start | bytes 6045704 | tf_op jit(solution)/shard_map/ppermute | solution.py:363
  28.2 21.2 %collective-permute-start.2 = (f32[5,328,128]{2,1,0:T(8,128)S(1)}, f32[5,328,128]{2,1,0:T(8,128)S(1)}, u32[]{:S(2)}, u32[]{:S(2)}) collective-permute-start(f32[5,328,128]{2,1,0:T(8,128)S(1)} %pad_maximum_fusion), channel_id=1, source_target_pairs={{0,248},{8,0},{16,8},{24,16},{32,24},{40,32},{48,40},{56,48},{64,5... | collective-permute-start | bytes 2519048 | tf_op jit(solution)/shard_map/ppermute | solution.py:355
  31.9 29.6 %collective-permute-start.3 = (f32[4,328,128]{2,1,0:T(8,128)S(1)}, f32[4,328,128]{2,1,0:T(8,128)S(1)}, u32[]{:S(2)}, u32[]{:S(2)}) collective-permute-start(f32[4,328,128]{2,1,0:T(8,128)S(1)} %fusion), channel_id=1, source_target_pairs={{0,8},{8,16},{16,24},{24,32},{32,40},{40,48},{48,56},{56,64},{64,7... | collective-permute-start | bytes 2015240 | tf_op jit(solution)/shard_map/ppermute | solution.py:355
  33.0 16.5 %collective-permute-start.6 = (f32[3,328,128]{2,1,0:T(8,128)S(1)}, f32[3,328,128]{2,1,0:T(8,128)S(1)}, u32[]{:S(2)}, u32[]{:S(2)}) collective-permute-start(f32[3,328,128]{2,1,0:T(8,128)S(1)} %get-tuple-element.64), channel_id=1, source_target_pairs={{0,6},{1,7},{2,0},{3,1},{4,2},{5,3},{6,4},{7,5},{8,14},{9,15},{10,... | collective-permute-start | bytes 1511432 | tf_op jit(solution)/shard_map/ppermute | solution.py:359
  35.8 13.7 %collective-permute-start.5 = (f32[3,328,128]{2,1,0:T(8,128)S(1)}, f32[3,328,128]{2,1,0:T(8,128)S(1)}, u32[]{:S(2)}, u32[]{:S(2)}) collective-permute-start(f32[3,328,128]{2,1,0:T(8,128)S(1)} %get-tuple-element.65), channel_id=1, source_target_pairs={{0,4},{1,5},{2,6},{3,7},{4,0},{5,1},{6,2},{7,3},{8,12},{9,13},{10,... | collective-permute-start | bytes 1511432 | tf_op jit(solution)/shard_map/ppermute | solution.py:359
  36.1 25.4 %collective-permute-start.4 = (f32[3,328,128]{2,1,0:T(8,128)S(1)}, f32[3,328,128]{2,1,0:T(8,128)S(1)}, u32[]{:S(2)}, u32[]{:S(2)}) collective-permute-start(f32[3,328,128]{2,1,0:T(8,128)S(1)} %get-tuple-element.66), channel_id=1, source_target_pairs={{0,2},{1,3},{2,4},{3,5},{4,6},{5,7},{6,0},{7,1},{8,10},{9,11},{10,... | collective-permute-start | bytes 1511432 | tf_op jit(solution)/shard_map/ppermute | solution.py:359
  61.6 11.7 %collective-permute-start.11 = (f32[8,328,128]{2,1,0:T(8,128)S(1)}, f32[8,328,128]{2,1,0:T(8,128)S(1)}, u32[]{:S(2)}, u32[]{:S(2)}) collective-permute-start(f32[8,328,128]{2,1,0:T(8,128)S(1)} %slice_dynamic-update-slice_fusion.1.mine), channel_id=1, source_target_pairs={{0,1},{1,0},{2,3},{3,2},{4,5},{5,4},{6,7},{7,6},{8,9},{9,8},{10,11... | collective-permute-start | bytes 4030472 | tf_op jit(solution)/shard_map/ppermute | solution.py:363
  62.3 9.3 %collective-permute-start.7 = (f32[328,128]{1,0:T(8,128)S(1)}, f32[328,128]{1,0:T(8,128)S(1)}, u32[]{:S(2)}, u32[]{:S(2)}) collective-permute-start(f32[328,128]{1,0:T(8,128)S(1)} %slice_bitcast_fusion.1), channel_id=1, source_target_pairs={{0,8},{8,16},{16,24},{24,32},{32,40},{40,48},{48,56},{56,64},{64,7... | collective-permute-start | bytes 503816 | tf_op jit(solution)/shard_map/ppermute | solution.py:355
  62.4 10.5 %collective-permute-start.10 = (f32[328,128]{1,0:T(8,128)S(1)}, f32[328,128]{1,0:T(8,128)S(1)}, u32[]{:S(2)}, u32[]{:S(2)}) collective-permute-start(f32[328,128]{1,0:T(8,128)S(1)} %slice_bitcast_fusion.2.rest_0_), channel_id=1, source_target_pairs={{0,2},{1,3},{2,4},{3,5},{4,6},{5,7},{6,0},{7,1},{8,10},{9,11},{10,... | collective-permute-start | bytes 503816 | tf_op jit(solution)/shard_map/ppermute | solution.py:359
  62.5 10.5 %collective-permute-start.9 = (f32[328,128]{1,0:T(8,128)S(1)}, f32[328,128]{1,0:T(8,128)S(1)}, u32[]{:S(2)}, u32[]{:S(2)}) collective-permute-start(f32[328,128]{1,0:T(8,128)S(1)} %slice_bitcast_fusion.2.rest_0_), channel_id=1, source_target_pairs={{0,4},{1,5},{2,6},{3,7},{4,0},{5,1},{6,2},{7,3},{8,12},{9,13},{10,... | collective-permute-start | bytes 503816 | tf_op jit(solution)/shard_map/ppermute | solution.py:359
  64.0 9.3 %collective-permute-start.8 = (f32[328,128]{1,0:T(8,128)S(1)}, f32[328,128]{1,0:T(8,128)S(1)}, u32[]{:S(2)}, u32[]{:S(2)}) collective-permute-start(f32[328,128]{1,0:T(8,128)S(1)} %slice_bitcast_fusion.2.rest_0_), channel_id=1, source_target_pairs={{0,6},{1,7},{2,0},{3,1},{4,2},{5,3},{6,4},{7,5},{8,14},{9,15},{10,... | collective-permute-start | bytes 503816 | tf_op jit(solution)/shard_map/ppermute | solution.py:359
  73.3 2.8 %collective-permute-start.12 = (f32[328,128]{1,0:T(8,128)S(1)}, f32[328,128]{1,0:T(8,128)S(1)}, u32[]{:S(2)}, u32[]{:S(2)}) collective-permute-start(f32[328,128]{1,0:T(8,128)S(1)} %slice_bitcast_fusion.2.rest_0_), channel_id=1, source_target_pairs={{0,1},{1,0},{2,3},{3,2},{4,5},{5,4},{6,7},{7,6},{8,9},{9,8},{10,11... | collective-permute-start | bytes 503816 | tf_op jit(solution)/shard_map/ppermute | solution.py:363
  74.6 1.5 %collective-permute-start.13 = (f32[328,128]{1,0:T(8,128)S(1)}, f32[328,128]{1,0:T(8,128)S(1)}, u32[]{:S(2)}, u32[]{:S(2)}) collective-permute-start(f32[328,128]{1,0:T(8,128)S(1)} %collective-permute-done.8.rest_1_), channel_id=1, source_target_pairs={{0,1},{1,0},{2,3},{3,2},{4,5},{5,4},{6,7},{7,6},{8,9},{9,8},{10,11... | collective-permute-start | bytes 503816 | tf_op jit(solution)/shard_map/ppermute | solution.py:363
  74.7 1.6 %collective-permute-start.14 = (f32[328,128]{1,0:T(8,128)S(1)}, f32[328,128]{1,0:T(8,128)S(1)}, u32[]{:S(2)}, u32[]{:S(2)}) collective-permute-start(f32[328,128]{1,0:T(8,128)S(1)} %collective-permute-done.9.rest_2_), channel_id=1, source_target_pairs={{0,1},{1,0},{2,3},{3,2},{4,5},{5,4},{6,7},{7,6},{8,9},{9,8},{10,11... | collective-permute-start | bytes 503816 | tf_op jit(solution)/shard_map/ppermute | solution.py:363
  75.2 1.4 %collective-permute-start.15 = (f32[328,128]{1,0:T(8,128)S(1)}, f32[328,128]{1,0:T(8,128)S(1)}, u32[]{:S(2)}, u32[]{:S(2)}) collective-permute-start(f32[328,128]{1,0:T(8,128)S(1)} %collective-permute-done.10.rest_3_), channel_id=1, source_target_pairs={{0,1},{1,0},{2,3},{3,2},{4,5},{5,4},{6,7},{7,6},{8,9},{9,8},{10,11... | collective-permute-start | bytes 503816 | tf_op jit(solution)/shard_map/ppermute | solution.py:363
  75.2 10.3 %collective-permute-start.16 = (f32[328,128]{1,0:T(8,128)S(1)}, f32[328,128]{1,0:T(8,128)S(1)}, u32[]{:S(2)}, u32[]{:S(2)}) collective-permute-start(f32[328,128]{1,0:T(8,128)S(1)} %fusion.20), channel_id=1, source_target_pairs={{0,16},{8,24},{16,32},{24,40},{32,48},{40,56},{48,64},{56,72},{64,... | collective-permute-start | bytes 503816 | tf_op jit(solution)/shard_map/ppermute | solution.py:355
  85.5 29.1 %copy-start.1 = (f32[8,256,256]{2,1,0:T(8,128)S(1)}, f32[8,256,256]{2,1,0:T(8,128)}, u32[]{:S(2)}) copy-start(f32[8,256,256]{2,1,0:T(8,128)} %transfer.1) | copy-start | bytes 6291460
  85.5 29.1 %copy-start.2 = (f32[2,256,256]{2,1,0:T(8,128)S(1)}, f32[2,256,256]{2,1,0:T(8,128)}, u32[]{:S(2)}) copy-start(f32[2,256,256]{2,1,0:T(8,128)} %upper.1) | copy-start | bytes 1572868
  85.5 4.6 %collective-permute-start.17 = (f32[4,328,128]{2,1,0:T(8,128)S(1)}, f32[4,328,128]{2,1,0:T(8,128)S(1)}, u32[]{:S(2)}, u32[]{:S(2)}) collective-permute-start(f32[4,328,128]{2,1,0:T(8,128)S(1)} %get-tuple-element.56), channel_id=1, source_target_pairs={{0,1},{1,0},{2,3},{3,2},{4,5},{5,4},{6,7},{7,6},{8,9},{9,8},{10,11... | collective-permute-start | bytes 2015240 | tf_op jit(solution)/shard_map/ppermute | solution.py:363
  90.2 6.8 %collective-permute-start.18 = (f32[328,128]{1,0:T(8,128)S(1)}, f32[328,128]{1,0:T(8,128)S(1)}, u32[]{:S(2)}, u32[]{:S(2)}) collective-permute-start(f32[328,128]{1,0:T(8,128)S(1)} %get-tuple-element.61), channel_id=1, source_target_pairs={{0,2},{1,3},{2,4},{3,5},{4,6},{5,7},{6,0},{7,1},{8,10},{9,11},{10,... | collective-permute-start | bytes 503816 | tf_op jit(solution)/shard_map/ppermute | solution.py:359
  90.3 6.7 %collective-permute-start.20 = (f32[328,128]{1,0:T(8,128)S(1)}, f32[328,128]{1,0:T(8,128)S(1)}, u32[]{:S(2)}, u32[]{:S(2)}) collective-permute-start(f32[328,128]{1,0:T(8,128)S(1)} %get-tuple-element.62), channel_id=1, source_target_pairs={{0,6},{1,7},{2,0},{3,1},{4,2},{5,3},{6,4},{7,5},{8,14},{9,15},{10,... | collective-permute-start | bytes 503816 | tf_op jit(solution)/shard_map/ppermute | solution.py:359
  93.0 8.2 %collective-permute-start.19 = (f32[328,128]{1,0:T(8,128)S(1)}, f32[328,128]{1,0:T(8,128)S(1)}, u32[]{:S(2)}, u32[]{:S(2)}) collective-permute-start(f32[328,128]{1,0:T(8,128)S(1)} %get-tuple-element.63), channel_id=1, source_target_pairs={{0,4},{1,5},{2,6},{3,7},{4,0},{5,1},{6,2},{7,3},{8,12},{9,13},{10,... | collective-permute-start | bytes 503816 | tf_op jit(solution)/shard_map/ppermute | solution.py:359
  101.2 5.9 %collective-permute-start.23 = (f32[328,128]{1,0:T(8,128)S(1)}, f32[328,128]{1,0:T(8,128)S(1)}, u32[]{:S(2)}, u32[]{:S(2)}) collective-permute-start(f32[328,128]{1,0:T(8,128)S(1)} %fusion.19.rest_0_), channel_id=1, source_target_pairs={{0,2},{1,3},{2,4},{3,5},{4,6},{5,7},{6,0},{7,1},{8,10},{9,11},{10,... | collective-permute-start | bytes 503816 | tf_op jit(solution)/shard_map/ppermute | solution.py:359
  101.9 9.1 %collective-permute-start.22 = (f32[328,128]{1,0:T(8,128)S(1)}, f32[328,128]{1,0:T(8,128)S(1)}, u32[]{:S(2)}, u32[]{:S(2)}) collective-permute-start(f32[328,128]{1,0:T(8,128)S(1)} %fusion.19.rest_0_), channel_id=1, source_target_pairs={{0,4},{1,5},{2,6},{3,7},{4,0},{5,1},{6,2},{7,3},{8,12},{9,13},{10,... | collective-permute-start | bytes 503816 | tf_op jit(solution)/shard_map/ppermute | solution.py:359
  104.3 8.8 %collective-permute-start.21 = (f32[328,128]{1,0:T(8,128)S(1)}, f32[328,128]{1,0:T(8,128)S(1)}, u32[]{:S(2)}, u32[]{:S(2)}) collective-permute-start(f32[328,128]{1,0:T(8,128)S(1)} %fusion.19.rest_0_), channel_id=1, source_target_pairs={{0,6},{1,7},{2,0},{3,1},{4,2},{5,3},{6,4},{7,5},{8,14},{9,15},{10,... | collective-permute-start | bytes 503816 | tf_op jit(solution)/shard_map/ppermute | solution.py:359
  104.3 9.1 %collective-permute-start.24 = (f32[328,128]{1,0:T(8,128)S(1)}, f32[328,128]{1,0:T(8,128)S(1)}, u32[]{:S(2)}, u32[]{:S(2)}) collective-permute-start(f32[328,128]{1,0:T(8,128)S(1)} %fusion.19.rest_0_), channel_id=1, source_target_pairs={{0,1},{1,0},{2,3},{3,2},{4,5},{5,4},{6,7},{7,6},{8,9},{9,8},{10,11... | collective-permute-start | bytes 503816 | tf_op jit(solution)/shard_map/ppermute | solution.py:363
  107.1 6.3 %collective-permute-start.27 = (f32[328,128]{1,0:T(8,128)S(1)}, f32[328,128]{1,0:T(8,128)S(1)}, u32[]{:S(2)}, u32[]{:S(2)}) collective-permute-start(f32[328,128]{1,0:T(8,128)S(1)} %collective-permute-done.23.rest_3_), channel_id=1, source_target_pairs={{0,1},{1,0},{2,3},{3,2},{4,5},{5,4},{6,7},{7,6},{8,9},{9,8},{10,11... | collective-permute-start | bytes 503816 | tf_op jit(solution)/shard_map/ppermute | solution.py:363
  111.0 3.2 %collective-permute-start.26 = (f32[328,128]{1,0:T(8,128)S(1)}, f32[328,128]{1,0:T(8,128)S(1)}, u32[]{:S(2)}, u32[]{:S(2)}) collective-permute-start(f32[328,128]{1,0:T(8,128)S(1)} %collective-permute-done.22.rest_2_), channel_id=1, source_target_pairs={{0,1},{1,0},{2,3},{3,2},{4,5},{5,4},{6,7},{7,6},{8,9},{9,8},{10,11... | collective-permute-start | bytes 503816 | tf_op jit(solution)/shard_map/ppermute | solution.py:363
  113.1 1.4 %collective-permute-start.25 = (f32[328,128]{1,0:T(8,128)S(1)}, f32[328,128]{1,0:T(8,128)S(1)}, u32[]{:S(2)}, u32[]{:S(2)}) collective-permute-start(f32[328,128]{1,0:T(8,128)S(1)} %collective-permute-done.21.rest_1_), channel_id=1, source_target_pairs={{0,1},{1,0},{2,3},{3,2},{4,5},{5,4},{6,7},{7,6},{8,9},{9,8},{10,11... | collective-permute-start | bytes 503816 | tf_op jit(solution)/shard_map/ppermute | solution.py:363

commit v2 on v1

--- a/solution.py
+++ b/solution.py
@@ -379,12 +379,10 @@
     parent_blocks,
 ):
     boxes, extent = child_basis.shape[0], child_basis.shape[-1]
-    where = jnp.concatenate(
+    early = jnp.concatenate(
         [
             jnp.stack([lax.axis_index("clus"), lax.axis_index("pair")]).astype(jnp.int32),
             child_parent.reshape(-1),
-            child_pairs.reshape(-1),
-            parent_pairs.reshape(-1),
         ]
     )
 
@@ -406,7 +404,10 @@
             pltpu.SemaphoreType.DMA((2, boxes // UNROLL)),
         ],
         16,
-    )(where, child_basis, transfer)
+    )(early, child_basis, transfer)
+
+    share, child_pairs, parent_pairs = lax.optimization_barrier((share, child_pairs, parent_pairs))
+    where = jnp.concatenate([early, child_pairs.reshape(-1), parent_pairs.reshape(-1)])
 
     second = to_clus(share, -2)
 

time: 119 us -> 123 us (1.034)
  waiting for transfers between devices: 46.2 us -> 49.4 us
  starting transfers between devices: 41.9 us -> 39.5 us
  local copies, waits for them, and re-layouts: 6.79 us -> 9.13 us
    ppermute x5, starting transfers between devices: 14.1 us -> 10.8 us  [to_clus(): lax.ppermute(value, 'clus', [(i, (i + steps) % count) for i in range(coun...]
    ppermute x11, waiting for transfers between devices: 3.78 us -> 6.94 us  [to_core(): return lax.ppermute(value, 'pair', [(i, i ^ 1) for i in range(PAIR)])]
    unnamed x20 -> x34, local copies, waits for them, and re-layouts: 5.85 us -> 8.67 us
  transfers between devices with their start and end apart: 28 -> 28, of which waited for: 15 -> 18; matrix products, arithmetic and copies ran while one was open for 0% -> 1% of each run, Pallas kernels for 12% -> 11%
where the time goes in v2:
time: 123 us
  waiting for transfers between devices  49.4 us (40%)
  starting transfers between devices  39.5 us (32%)
  Pallas kernels  22.5 us (18%)
  local copies, waits for them, and re-layouts  9.13 us (7%)
  other arithmetic  1.46 us (1%)
    ppermute x12, waiting for transfers between devices, to_y(): lax.ppermute(value, 'pair', [(i, (i + 2 * steps) % PAIR) for i in range(P...  22.9 us
    ppermute x5, waiting for transfers between devices, to_clus(): lax.ppermute(value, 'clus', [(i, (i + steps) % count) for i in range(coun...  19.6 us
    ppermute x11, starting transfers between devices, to_core(): return lax.ppermute(value, 'pair', [(i, i ^ 1) for i in range(PAIR)])  15.6 us
    ppermute x12, starting transfers between devices, to_y(): lax.ppermute(value, 'pair', [(i, (i + 2 * steps) % PAIR) for i in range(P...  13 us
    ppermute x5, starting transfers between devices, to_clus(): lax.ppermute(value, 'clus', [(i, (i + steps) % count) for i in range(coun...  10.8 us
    unnamed x34, local copies, waits for them, and re-layouts  8.67 us
    pallas_call x1, Pallas kernels, per_device(): call(near_kernel, 'near', (floats(4, SHARE, HALF), floats(4, SHARE, HALF)...  7.48 us
    ppermute x11, waiting for transfers between devices, to_core(): return lax.ppermute(value, 'pair', [(i, i ^ 1) for i in range(PAIR)])  6.94 us
  transfers between devices with their start and end apart: 28, of which 18 were waited for; matrix products, arithmetic and copies ran while one was open for 1% of the time, Pallas kernels for 11%

profile of v2, /device:TPU:1, one launch (start us, length us, event | category | flops | bytes accessed | tf_op | source)
XLA Modules:
  0.0 122.7 jit_solution(2027510725889408615)
XLA Ops:
  0.6 0.7 pad_add_fusion.where
  1.4 1.6 %copy-done = f32[8,256,256]{2,1,0:T(8,128)S(1)} copy-done((f32[8,256,256]{2,1,0:T(8,128)S(1)}, f32[8,256,256]{2,1,0:T(8,128)}, u32[]{:S(2)}) %copy-start) | copy-done | bytes 2097176
  3.0 1.6 %copy-done.5 = f32[8,256,256]{2,1,0:T(8,128)S(1)} copy-done((f32[8,256,256]{2,1,0:T(8,128)S(1)}, f32[8,256,256]{2,1,0:T(8,128)}, u32[]{:S(2)}) %copy-start.5) | copy-done | bytes 2097176
  4.6 4.0 %lift.1 = (f32[2,256,256]{2,1,0:T(8,128)}, f32[4,328,128]{2,1,0:T(8,128)S(1)}, f32[4,328,128]{2,1,0:T(8,128)S(1)}, f32[328,128]{1,0:T(8,128)S(1)}) custom-call(s32[10]{0:T(128)S(1)} %pad_add_fusion.where, f32[8,256,256]{2,1,0:T(8,128)S(1)} %copy-done.5, f32[8,256,256]{2,1,0:T(8,128)S(1)} %copy-done), custom_call_target="tpu_custom_call" | custom-call | flops 1610612736 | bytes 8388608 | tf_op jit(solution)/shard_map/lift/pallas_call | solution.py:389
  8.6 0.8 copy-done.10
  9.5 9.0 %collective-permute-start = (f32[328,128]{1,0:T(8,128)S(1)}, f32[328,128]{1,0:T(8,128)S(1)}, u32[]{:S(2)}, u32[]{:S(2)}) collective-permute-start(f32[328,128]{1,0:T(8,128)S(1)} %get-tuple-element.36), channel_id=1, source_target_pairs={{0,240},{8,248},{16,0},{24,8},{32,16},{40,24},{48,32},{56,40},{64,... | collective-permute-start | bytes 503816 | tf_op jit(solution)/shard_map/ppermute | solution.py:355
  18.5 0.1 copy.13
  18.6 0.1 reshape.28
  18.7 0.1 copy.12
  18.8 0.1 reshape.27
  19.0 1.9 %copy-done.3 = f32[12,256,256]{2,1,0:T(8,128)S(1)} copy-done((f32[12,256,256]{2,1,0:T(8,128)S(1)}, f32[12,256,256]{2,1,0:T(8,128)}, u32[]{:S(2)}) %copy-start.3) | copy-done | bytes 3145752
  20.8 1.6 %copy-done.7 = f32[8,256,256]{2,1,0:T(8,128)S(1)} copy-done((f32[8,256,256]{2,1,0:T(8,128)S(1)}, f32[8,256,256]{2,1,0:T(8,128)}, u32[]{:S(2)}) %copy-start.7) | copy-done | bytes 2097176
  22.4 1.0 copy-done.9
  23.5 6.6 %far.1 = (f32[4,3,328,128]{3,2,1,0:T(8,128)S(1)}, f32[4,3,328,128]{3,2,1,0:T(8,128)S(1)}, f32[8,328,128]{2,1,0:T(8,128)S(1)}) custom-call(s32[50]{0:T(128)S(1)} %concatenate.23.where, f32[8,256,256]{2,1,0:T(8,128)S(1)} %copy-done.6, f32[2,256,256]{2,1,0:T(8,128)S(1)} %copy-done.9, f32[12,256,256]{2,1,0:T(8,128)S(1)} %copy-done.3, f32[8,256,256]{2,1,0:T(8,128)S(1)} %copy-done.7), custom_call_target="tpu_custom_call" | custom-call | flops 4026531840 | bytes 8388608 | tf_op jit(solution)/shard_map/far/pallas_call | solution.py:414
  30.1 1.0 collective-permute-start.1
  31.2 0.8 collective-permute-start.2
  32.0 2.8 %collective-permute-done.1 = f32[4,3,328,128]{3,2,1,0:T(8,128)S(1)} collective-permute-done((f32[4,3,328,128]{3,2,1,0:T(8,128)S(1)}, f32[4,3,328,128]{3,2,1,0:T(8,128)S(1)}, u32[]{:S(2)}, u32[]{:S(2)}) %collective-permute-start.1) | collective-permute-done | bytes 2015264 | tf_op jit(solution)/shard_map/ppermute | solution.py:363
  34.8 0.1 fusion
  34.9 0.8 collective-permute-start.3
  35.7 0.1 fusion.1
  35.8 0.1 pad_maximum_fusion.1
  35.9 2.8 %collective-permute-start.6 = (f32[3,328,128]{2,1,0:T(8,128)S(1)}, f32[3,328,128]{2,1,0:T(8,128)S(1)}, u32[]{:S(2)}, u32[]{:S(2)}) collective-permute-start(f32[3,328,128]{2,1,0:T(8,128)S(1)} %get-tuple-element.70), channel_id=1, source_target_pairs={{0,6},{1,7},{2,0},{3,1},{4,2},{5,3},{6,4},{7,5},{8,14},{9,15},{10,... | collective-permute-start | bytes 1511432 | tf_op jit(solution)/shard_map/ppermute | solution.py:359
  38.8 0.3 collective-permute-start.5
  39.1 0.7 collective-permute-start.4
  39.8 11.8 %collective-permute-done.2 = f32[5,328,128]{2,1,0:T(8,128)S(1)} collective-permute-done((f32[5,328,128]{2,1,0:T(8,128)S(1)}, f32[5,328,128]{2,1,0:T(8,128)S(1)}, u32[]{:S(2)}, u32[]{:S(2)}) %collective-permute-start.2) | collective-permute-done | bytes 839712 | tf_op jit(solution)/shard_map/ppermute | solution.py:355
  51.6 0.8 collective-permute-done.5
  52.4 12.1 %collective-permute-done.4 = f32[3,328,128]{2,1,0:T(8,128)S(1)} collective-permute-done((f32[3,328,128]{2,1,0:T(8,128)S(1)}, f32[3,328,128]{2,1,0:T(8,128)S(1)}, u32[]{:S(2)}, u32[]{:S(2)}) %collective-permute-start.4) | collective-permute-done | bytes 503840 | tf_op jit(solution)/shard_map/ppermute | solution.py:359
  64.6 0.6 collective-permute-start.11
  65.2 0.1 fusion.7
  65.4 0.1 collective-permute-start.7
  65.4 0.1 collective-permute-start.10
  65.5 1.5 %collective-permute-start.9 = (f32[328,128]{1,0:T(8,128)S(1)}, f32[328,128]{1,0:T(8,128)S(1)}, u32[]{:S(2)}, u32[]{:S(2)}) collective-permute-start(f32[328,128]{1,0:T(8,128)S(1)} %slice_bitcast_fusion.2.rest_0_), channel_id=1, source_target_pairs={{0,4},{1,5},{2,6},{3,7},{4,0},{5,1},{6,2},{7,3},{8,12},{9,13},{10,... | collective-permute-start | bytes 503816 | tf_op jit(solution)/shard_map/ppermute | solution.py:359
  67.0 1.2 collective-permute-start.8
  68.2 6.4 %collective-permute-done.7.after = f32[328,128]{1,0:T(8,128)S(1)} collective-permute-done((f32[328,128]{1,0:T(8,128)S(1)}, f32[328,128]{1,0:T(8,128)S(1)}, u32[]{:S(2)}, u32[]{:S(2)}) %collective-permute-start.7) | collective-permute-done | bytes 167968 | tf_op jit(solution)/shard_map/ppermute | solution.py:355
  74.6 1.3 %collective-permute-done.10.rest_3_ = f32[328,128]{1,0:T(8,128)S(1)} collective-permute-done((f32[328,128]{1,0:T(8,128)S(1)}, f32[328,128]{1,0:T(8,128)S(1)}, u32[]{:S(2)}, u32[]{:S(2)}) %collective-permute-start.10) | collective-permute-done | bytes 167968 | tf_op jit(solution)/shard_map/ppermute | solution.py:359
  76.0 0.3 collective-permute-done.8.rest_1_
  76.3 1.4 %collective-permute-start.12 = (f32[328,128]{1,0:T(8,128)S(1)}, f32[328,128]{1,0:T(8,128)S(1)}, u32[]{:S(2)}, u32[]{:S(2)}) collective-permute-start(f32[328,128]{1,0:T(8,128)S(1)} %slice_bitcast_fusion.2.rest_0_), channel_id=1, source_target_pairs={{0,1},{1,0},{2,3},{3,2},{4,5},{5,4},{6,7},{7,6},{8,9},{9,8},{10,11... | collective-permute-start | bytes 503816 | tf_op jit(solution)/shard_map/ppermute | solution.py:363
  77.7 0.5 collective-permute-start.14
  78.2 0.1 collective-permute-start.16
  78.3 0.4 collective-permute-done.12.rest_4_
  78.7 0.4 collective-permute-done.13.rest_5_
  79.1 0.2 collective-permute-done.14.rest_6_
  79.3 0.3 collective-permute-done.15.rest_7_
  79.6 7.5 %near.1 = (f32[4,328,128]{2,1,0:T(8,128)S(1)}, f32[4,328,128]{2,1,0:T(8,128)S(1)}) custom-call(s32[50]{0:T(128)S(1)} %concatenate.23.where, f32[328,128]{1,0:T(8,128)S(1)} %collective-permute-done.7.after, f32[4,328,128]{2,1,0:T(8,128)S(1)} %collective-permute-done.3.also_after, f32[12,256,256]{2,1,0:T(8,128)S(1)} %copy-done.4, ...), custom_call_target="tpu_custom_call" | custom-call | flops 4026531840 | bytes 8388608 | tf_op jit(solution)/shard_map/near/pallas_call | solution.py:454
  87.1 1.4 %collective-permute-done.16 = f32[328,128]{1,0:T(8,128)S(1)} collective-permute-done((f32[328,128]{1,0:T(8,128)S(1)}, f32[328,128]{1,0:T(8,128)S(1)}, u32[]{:S(2)}, u32[]{:S(2)}) %collective-permute-start.16) | collective-permute-done | bytes 167968 | tf_op jit(solution)/shard_map/ppermute | solution.py:355
  88.4 3.8 %collective-permute-start.17 = (f32[4,328,128]{2,1,0:T(8,128)S(1)}, f32[4,328,128]{2,1,0:T(8,128)S(1)}, u32[]{:S(2)}, u32[]{:S(2)}) collective-permute-start(f32[4,328,128]{2,1,0:T(8,128)S(1)} %get-tuple-element.62), channel_id=1, source_target_pairs={{0,1},{1,0},{2,3},{3,2},{4,5},{5,4},{6,7},{7,6},{8,9},{9,8},{10,11... | collective-permute-start | bytes 2015240 | tf_op jit(solution)/shard_map/ppermute | solution.py:363
  92.2 1.7 %collective-permute-done.17 = f32[4,328,128]{2,1,0:T(8,128)S(1)} collective-permute-done((f32[4,328,128]{2,1,0:T(8,128)S(1)}, f32[4,328,128]{2,1,0:T(8,128)S(1)}, u32[]{:S(2)}, u32[]{:S(2)}) %collective-permute-start.17) | collective-permute-done | bytes 671776 | tf_op jit(solution)/shard_map/ppermute | solution.py:363
  93.9 0.1 fusion.13
  94.0 0.1 collective-permute-start.18
  94.1 2.7 %collective-permute-start.20 = (f32[328,128]{1,0:T(8,128)S(1)}, f32[328,128]{1,0:T(8,128)S(1)}, u32[]{:S(2)}, u32[]{:S(2)}) collective-permute-start(f32[328,128]{1,0:T(8,128)S(1)} %get-tuple-element.68), channel_id=1, source_target_pairs={{0,6},{1,7},{2,0},{3,1},{4,2},{5,3},{6,4},{7,5},{8,14},{9,15},{10,... | collective-permute-start | bytes 503816 | tf_op jit(solution)/shard_map/ppermute | solution.py:359
  96.8 0.6 collective-permute-start.19
  97.4 3.5 %collective-permute-done.18 = f32[328,128]{1,0:T(8,128)S(1)} collective-permute-done((f32[328,128]{1,0:T(8,128)S(1)}, f32[328,128]{1,0:T(8,128)S(1)}, u32[]{:S(2)}, u32[]{:S(2)}) %collective-permute-start.18) | collective-permute-done | bytes 167968 | tf_op jit(solution)/shard_map/ppermute | solution.py:359
  100.8 4.2 %collective-permute-done.19 = f32[328,128]{1,0:T(8,128)S(1)} collective-permute-done((f32[328,128]{1,0:T(8,128)S(1)}, f32[328,128]{1,0:T(8,128)S(1)}, u32[]{:S(2)}, u32[]{:S(2)}) %collective-permute-start.19) | collective-permute-done | bytes 167968 | tf_op jit(solution)/shard_map/ppermute | solution.py:359
  105.0 0.1 fusion.19.rest_0_
  105.1 0.6 collective-permute-start.23
  105.7 2.4 %collective-permute-start.22 = (f32[328,128]{1,0:T(8,128)S(1)}, f32[328,128]{1,0:T(8,128)S(1)}, u32[]{:S(2)}, u32[]{:S(2)}) collective-permute-start(f32[328,128]{1,0:T(8,128)S(1)} %fusion.19.rest_0_), channel_id=1, source_target_pairs={{0,4},{1,5},{2,6},{3,7},{4,0},{5,1},{6,2},{7,3},{8,12},{9,13},{10,... | collective-permute-start | bytes 503816 | tf_op jit(solution)/shard_map/ppermute | solution.py:359
  108.2 2.1 %collective-permute-start.24 = (f32[328,128]{1,0:T(8,128)S(1)}, f32[328,128]{1,0:T(8,128)S(1)}, u32[]{:S(2)}, u32[]{:S(2)}) collective-permute-start(f32[328,128]{1,0:T(8,128)S(1)} %fusion.19.rest_0_), channel_id=1, source_target_pairs={{0,1},{1,0},{2,3},{3,2},{4,5},{5,4},{6,7},{7,6},{8,9},{9,8},{10,11... | collective-permute-start | bytes 503816 | tf_op jit(solution)/shard_map/ppermute | solution.py:363
  110.3 0.7 collective-permute-done.23.rest_3_
  110.9 3.9 %collective-permute-start.27 = (f32[328,128]{1,0:T(8,128)S(1)}, f32[328,128]{1,0:T(8,128)S(1)}, u32[]{:S(2)}, u32[]{:S(2)}) collective-permute-start(f32[328,128]{1,0:T(8,128)S(1)} %collective-permute-done.23.rest_3_), channel_id=1, source_target_pairs={{0,1},{1,0},{2,3},{3,2},{4,5},{5,4},{6,7},{7,6},{8,9},{9,8},{10,11... | collective-permute-start | bytes 503816 | tf_op jit(solution)/shard_map/ppermute | solution.py:363
  114.8 2.1 %collective-permute-start.26 = (f32[328,128]{1,0:T(8,128)S(1)}, f32[328,128]{1,0:T(8,128)S(1)}, u32[]{:S(2)}, u32[]{:S(2)}) collective-permute-start(f32[328,128]{1,0:T(8,128)S(1)} %collective-permute-done.22.rest_2_), channel_id=1, source_target_pairs={{0,1},{1,0},{2,3},{3,2},{4,5},{5,4},{6,7},{7,6},{8,9},{9,8},{10,11... | collective-permute-start | bytes 503816 | tf_op jit(solution)/shard_map/ppermute | solution.py:363
  117.0 0.3 collective-permute-start.25
  117.3 0.7 collective-permute-done.26.rest_6_
  118.0 0.4 collective-permute-done.25.rest_5_
  118.4 4.4 %lower.1 = f32[8,256,256]{2,1,0:T(8,128)} custom-call(s32[50]{0:T(128)S(1)} %concatenate.23.where, f32[8,256,256]{2,1,0:T(8,128)S(1)} %copy-done.1, f32[2,256,256]{2,1,0:T(8,128)S(1)} %copy-done.2, f32[328,128]{1,0:T(8,128)S(1)} %fusion.19.rest_0_, f32[328,128]{1,0:T(8,128)S(1)} %collective-permute-done.21.rest_1_, ...), custom_call_target="tpu_custom_call" | custom-call | flops 1610612736 | bytes 8388608 | tf_op jit(solution)/shard_map/lower/pallas_call | solution.py:478
  (47 shorter events, 0.4 us)
Async XLA Ops:
  1.4 1.6 %copy-start = (f32[8,256,256]{2,1,0:T(8,128)S(1)}, f32[8,256,256]{2,1,0:T(8,128)}, u32[]{:S(2)}) copy-start(f32[8,256,256]{2,1,0:T(8,128)} %transfer.1) | copy-start | bytes 6291460
  3.0 1.6 %copy-start.5 = (f32[8,256,256]{2,1,0:T(8,128)S(1)}, f32[8,256,256]{2,1,0:T(8,128)}, u32[]{:S(2)}) copy-start(f32[8,256,256]{2,1,0:T(8,128)} %child_basis.1) | copy-start | bytes 6291460
  4.6 14.0 %copy-start.13 = (s32[8,2]{0,1:T(2,128)S(1)}, s32[8,2]{0,1:T(2,128)}, u32[]{:S(2)}) copy-start(s32[8,2]{0,1:T(2,128)} %param.14) | copy-start | bytes 196
  4.6 14.1 %copy-start.14 = (s32[12,2]{0,1:T(2,128)S(1)}, s32[12,2]{0,1:T(2,128)}, u32[]{:S(2)}) copy-start(s32[12,2]{0,1:T(2,128)} %param.12) | copy-start | bytes 292
  4.6 14.3 %copy-start.12 = (s32[1,8]{1,0:T(1,128)S(1)}, s32[1,8]{1,0:T(1,128)}, u32[]{:S(2)}) copy-start(s32[1,8]{1,0:T(1,128)} %param.10) | copy-start | bytes 100
  4.6 14.4 %copy-start.6 = (f32[8,256,256]{2,1,0:T(8,128)S(1)}, f32[8,256,256]{2,1,0:T(8,128)}, u32[]{:S(2)}) copy-start(f32[8,256,256]{2,1,0:T(8,128)} %child_basis.1) | copy-start | bytes 6291460
  8.6 0.8 copy-start.10
  9.5 20.6 %collective-permute-start = (f32[328,128]{1,0:T(8,128)S(1)}, f32[328,128]{1,0:T(8,128)S(1)}, u32[]{:S(2)}, u32[]{:S(2)}) collective-permute-start(f32[328,128]{1,0:T(8,128)S(1)} %get-tuple-element.36), channel_id=1, source_target_pairs={{0,240},{8,248},{16,0},{24,8},{32,16},{40,24},{48,32},{56,40},{64,... | collective-permute-start | bytes 503816 | tf_op jit(solution)/shard_map/ppermute | solution.py:355
  18.9 1.9 %copy-start.3 = (f32[12,256,256]{2,1,0:T(8,128)S(1)}, f32[12,256,256]{2,1,0:T(8,128)}, u32[]{:S(2)}) copy-start(f32[12,256,256]{2,1,0:T(8,128)} %child_blocks.3) | copy-start | bytes 9437188
  20.8 1.6 %copy-start.7 = (f32[8,256,256]{2,1,0:T(8,128)S(1)}, f32[8,256,256]{2,1,0:T(8,128)}, u32[]{:S(2)}) copy-start(f32[8,256,256]{2,1,0:T(8,128)} %parent_blocks.3) | copy-start | bytes 6291460
  22.4 1.0 copy-start.9
  30.1 4.7 %collective-permute-start.1 = (f32[4,3,328,128]{3,2,1,0:T(8,128)S(1)}, f32[4,3,328,128]{3,2,1,0:T(8,128)S(1)}, u32[]{:S(2)}, u32[]{:S(2)}) collective-permute-start(f32[4,3,328,128]{3,2,1,0:T(8,128)S(1)} %get-tuple-element.42), channel_id=1, source_target_pairs={{0,1},{1,0},{2,3},{3,2},{4,5},{5,4},{6,7},{7,6},{8,9},{9,8},{10,11... | collective-permute-start | bytes 6045704 | tf_op jit(solution)/shard_map/ppermute | solution.py:363
  31.2 20.4 %collective-permute-start.2 = (f32[5,328,128]{2,1,0:T(8,128)S(1)}, f32[5,328,128]{2,1,0:T(8,128)S(1)}, u32[]{:S(2)}, u32[]{:S(2)}) collective-permute-start(f32[5,328,128]{2,1,0:T(8,128)S(1)} %pad_maximum_fusion), channel_id=1, source_target_pairs={{0,248},{8,0},{16,8},{24,16},{32,24},{40,32},{48,40},{56,48},{64,5... | collective-permute-start | bytes 2519048 | tf_op jit(solution)/shard_map/ppermute | solution.py:355
  34.9 29.6 %collective-permute-start.3 = (f32[4,328,128]{2,1,0:T(8,128)S(1)}, f32[4,328,128]{2,1,0:T(8,128)S(1)}, u32[]{:S(2)}, u32[]{:S(2)}) collective-permute-start(f32[4,328,128]{2,1,0:T(8,128)S(1)} %fusion), channel_id=1, source_target_pairs={{0,8},{8,16},{16,24},{24,32},{32,40},{40,48},{48,56},{56,64},{64,7... | collective-permute-start | bytes 2015240 | tf_op jit(solution)/shard_map/ppermute | solution.py:355
  35.8 43.8 %copy-start.11 = (f32[4,328,128]{2,1,0:T(8,128)S(1)}, f32[4,328,128]{2,1,0:T(8,128)}, u32[]{:S(2)}) copy-start(f32[4,328,128]{2,1,0:T(8,128)} %copy-done.10) | copy-start | bytes 2015236
  35.9 15.6 %collective-permute-start.6 = (f32[3,328,128]{2,1,0:T(8,128)S(1)}, f32[3,328,128]{2,1,0:T(8,128)S(1)}, u32[]{:S(2)}, u32[]{:S(2)}) collective-permute-start(f32[3,328,128]{2,1,0:T(8,128)S(1)} %get-tuple-element.70), channel_id=1, source_target_pairs={{0,6},{1,7},{2,0},{3,1},{4,2},{5,3},{6,4},{7,5},{8,14},{9,15},{10,... | collective-permute-start | bytes 1511432 | tf_op jit(solution)/shard_map/ppermute | solution.py:359
  38.8 13.6 %collective-permute-start.5 = (f32[3,328,128]{2,1,0:T(8,128)S(1)}, f32[3,328,128]{2,1,0:T(8,128)S(1)}, u32[]{:S(2)}, u32[]{:S(2)}) collective-permute-start(f32[3,328,128]{2,1,0:T(8,128)S(1)} %get-tuple-element.71), channel_id=1, source_target_pairs={{0,4},{1,5},{2,6},{3,7},{4,0},{5,1},{6,2},{7,3},{8,12},{9,13},{10,... | collective-permute-start | bytes 1511432 | tf_op jit(solution)/shard_map/ppermute | solution.py:359
  39.1 25.4 %collective-permute-start.4 = (f32[3,328,128]{2,1,0:T(8,128)S(1)}, f32[3,328,128]{2,1,0:T(8,128)S(1)}, u32[]{:S(2)}, u32[]{:S(2)}) collective-permute-start(f32[3,328,128]{2,1,0:T(8,128)S(1)} %get-tuple-element.72), channel_id=1, source_target_pairs={{0,2},{1,3},{2,4},{3,5},{4,6},{5,7},{6,0},{7,1},{8,10},{9,11},{10,... | collective-permute-start | bytes 1511432 | tf_op jit(solution)/shard_map/ppermute | solution.py:359
  64.5 15.1 %copy-start.8 = (f32[8,256,256]{2,1,0:T(8,128)S(1)}, f32[8,256,256]{2,1,0:T(8,128)}, u32[]{:S(2)}) copy-start(f32[8,256,256]{2,1,0:T(8,128)} %parent_blocks.3) | copy-start | bytes 6291460
  64.6 11.7 %collective-permute-start.11 = (f32[8,328,128]{2,1,0:T(8,128)S(1)}, f32[8,328,128]{2,1,0:T(8,128)S(1)}, u32[]{:S(2)}, u32[]{:S(2)}) collective-permute-start(f32[8,328,128]{2,1,0:T(8,128)S(1)} %slice_dynamic-update-slice_fusion.1.mine), channel_id=1, source_target_pairs={{0,1},{1,0},{2,3},{3,2},{4,5},{5,4},{6,7},{7,6},{8,9},{9,8},{10,11... | collective-permute-start | bytes 4030472 | tf_op jit(solution)/shard_map/ppermute | solution.py:363
  65.2 14.4 %copy-start.4 = (f32[12,256,256]{2,1,0:T(8,128)S(1)}, f32[12,256,256]{2,1,0:T(8,128)}, u32[]{:S(2)}) copy-start(f32[12,256,256]{2,1,0:T(8,128)} %child_blocks.3) | copy-start | bytes 9437188
  65.4 9.3 %collective-permute-start.7 = (f32[328,128]{1,0:T(8,128)S(1)}, f32[328,128]{1,0:T(8,128)S(1)}, u32[]{:S(2)}, u32[]{:S(2)}) collective-permute-start(f32[328,128]{1,0:T(8,128)S(1)} %slice_bitcast_fusion.1), channel_id=1, source_target_pairs={{0,8},{8,16},{16,24},{24,32},{32,40},{40,48},{48,56},{56,64},{64,7... | collective-permute-start | bytes 503816 | tf_op jit(solution)/shard_map/ppermute | solution.py:355
  65.4 10.5 %collective-permute-start.10 = (f32[328,128]{1,0:T(8,128)S(1)}, f32[328,128]{1,0:T(8,128)S(1)}, u32[]{:S(2)}, u32[]{:S(2)}) collective-permute-start(f32[328,128]{1,0:T(8,128)S(1)} %slice_bitcast_fusion.2.rest_0_), channel_id=1, source_target_pairs={{0,2},{1,3},{2,4},{3,5},{4,6},{5,7},{6,0},{7,1},{8,10},{9,11},{10,... | collective-permute-start | bytes 503816 | tf_op jit(solution)/shard_map/ppermute | solution.py:359
  65.5 10.5 %collective-permute-start.9 = (f32[328,128]{1,0:T(8,128)S(1)}, f32[328,128]{1,0:T(8,128)S(1)}, u32[]{:S(2)}, u32[]{:S(2)}) collective-permute-start(f32[328,128]{1,0:T(8,128)S(1)} %slice_bitcast_fusion.2.rest_0_), channel_id=1, source_target_pairs={{0,4},{1,5},{2,6},{3,7},{4,0},{5,1},{6,2},{7,3},{8,12},{9,13},{10,... | collective-permute-start | bytes 503816 | tf_op jit(solution)/shard_map/ppermute | solution.py:359
  67.0 9.3 %collective-permute-start.8 = (f32[328,128]{1,0:T(8,128)S(1)}, f32[328,128]{1,0:T(8,128)S(1)}, u32[]{:S(2)}, u32[]{:S(2)}) collective-permute-start(f32[328,128]{1,0:T(8,128)S(1)} %slice_bitcast_fusion.2.rest_0_), channel_id=1, source_target_pairs={{0,6},{1,7},{2,0},{3,1},{4,2},{5,3},{6,4},{7,5},{8,14},{9,15},{10,... | collective-permute-start | bytes 503816 | tf_op jit(solution)/shard_map/ppermute | solution.py:359
  76.3 2.4 %collective-permute-start.12 = (f32[328,128]{1,0:T(8,128)S(1)}, f32[328,128]{1,0:T(8,128)S(1)}, u32[]{:S(2)}, u32[]{:S(2)}) collective-permute-start(f32[328,128]{1,0:T(8,128)S(1)} %slice_bitcast_fusion.2.rest_0_), channel_id=1, source_target_pairs={{0,1},{1,0},{2,3},{3,2},{4,5},{5,4},{6,7},{7,6},{8,9},{9,8},{10,11... | collective-permute-start | bytes 503816 | tf_op jit(solution)/shard_map/ppermute | solution.py:363
  77.7 1.4 %collective-permute-start.13 = (f32[328,128]{1,0:T(8,128)S(1)}, f32[328,128]{1,0:T(8,128)S(1)}, u32[]{:S(2)}, u32[]{:S(2)}) collective-permute-start(f32[328,128]{1,0:T(8,128)S(1)} %collective-permute-done.8.rest_1_), channel_id=1, source_target_pairs={{0,1},{1,0},{2,3},{3,2},{4,5},{5,4},{6,7},{7,6},{8,9},{9,8},{10,11... | collective-permute-start | bytes 503816 | tf_op jit(solution)/shard_map/ppermute | solution.py:363
  77.7 1.6 %collective-permute-start.14 = (f32[328,128]{1,0:T(8,128)S(1)}, f32[328,128]{1,0:T(8,128)S(1)}, u32[]{:S(2)}, u32[]{:S(2)}) collective-permute-start(f32[328,128]{1,0:T(8,128)S(1)} %collective-permute-done.9.rest_2_), channel_id=1, source_target_pairs={{0,1},{1,0},{2,3},{3,2},{4,5},{5,4},{6,7},{7,6},{8,9},{9,8},{10,11... | collective-permute-start | bytes 503816 | tf_op jit(solution)/shard_map/ppermute | solution.py:363
  78.2 1.4 %collective-permute-start.15 = (f32[328,128]{1,0:T(8,128)S(1)}, f32[328,128]{1,0:T(8,128)S(1)}, u32[]{:S(2)}, u32[]{:S(2)}) collective-permute-start(f32[328,128]{1,0:T(8,128)S(1)} %collective-permute-done.10.rest_3_), channel_id=1, source_target_pairs={{0,1},{1,0},{2,3},{3,2},{4,5},{5,4},{6,7},{7,6},{8,9},{9,8},{10,11... | collective-permute-start | bytes 503816 | tf_op jit(solution)/shard_map/ppermute | solution.py:363
  78.2 10.2 %collective-permute-start.16 = (f32[328,128]{1,0:T(8,128)S(1)}, f32[328,128]{1,0:T(8,128)S(1)}, u32[]{:S(2)}, u32[]{:S(2)}) collective-permute-start(f32[328,128]{1,0:T(8,128)S(1)} %fusion.20), channel_id=1, source_target_pairs={{0,16},{8,24},{16,32},{24,40},{32,48},{40,56},{48,64},{56,72},{64,... | collective-permute-start | bytes 503816 | tf_op jit(solution)/shard_map/ppermute | solution.py:355
  88.4 29.9 %copy-start.1 = (f32[8,256,256]{2,1,0:T(8,128)S(1)}, f32[8,256,256]{2,1,0:T(8,128)}, u32[]{:S(2)}) copy-start(f32[8,256,256]{2,1,0:T(8,128)} %transfer.1) | copy-start | bytes 6291460
  88.4 29.9 %copy-start.2 = (f32[2,256,256]{2,1,0:T(8,128)S(1)}, f32[2,256,256]{2,1,0:T(8,128)}, u32[]{:S(2)}) copy-start(f32[2,256,256]{2,1,0:T(8,128)} %upper.1) | copy-start | bytes 1572868
  88.4 5.5 %collective-permute-start.17 = (f32[4,328,128]{2,1,0:T(8,128)S(1)}, f32[4,328,128]{2,1,0:T(8,128)S(1)}, u32[]{:S(2)}, u32[]{:S(2)}) collective-permute-start(f32[4,328,128]{2,1,0:T(8,128)S(1)} %get-tuple-element.62), channel_id=1, source_target_pairs={{0,1},{1,0},{2,3},{3,2},{4,5},{5,4},{6,7},{7,6},{8,9},{9,8},{10,11... | collective-permute-start | bytes 2015240 | tf_op jit(solution)/shard_map/ppermute | solution.py:363
  94.0 6.8 %collective-permute-start.18 = (f32[328,128]{1,0:T(8,128)S(1)}, f32[328,128]{1,0:T(8,128)S(1)}, u32[]{:S(2)}, u32[]{:S(2)}) collective-permute-start(f32[328,128]{1,0:T(8,128)S(1)} %get-tuple-element.67), channel_id=1, source_target_pairs={{0,2},{1,3},{2,4},{3,5},{4,6},{5,7},{6,0},{7,1},{8,10},{9,11},{10,... | collective-permute-start | bytes 503816 | tf_op jit(solution)/shard_map/ppermute | solution.py:359
  94.1 6.7 %collective-permute-start.20 = (f32[328,128]{1,0:T(8,128)S(1)}, f32[328,128]{1,0:T(8,128)S(1)}, u32[]{:S(2)}, u32[]{:S(2)}) collective-permute-start(f32[328,128]{1,0:T(8,128)S(1)} %get-tuple-element.68), channel_id=1, source_target_pairs={{0,6},{1,7},{2,0},{3,1},{4,2},{5,3},{6,4},{7,5},{8,14},{9,15},{10,... | collective-permute-start | bytes 503816 | tf_op jit(solution)/shard_map/ppermute | solution.py:359
  96.8 8.2 %collective-permute-start.19 = (f32[328,128]{1,0:T(8,128)S(1)}, f32[328,128]{1,0:T(8,128)S(1)}, u32[]{:S(2)}, u32[]{:S(2)}) collective-permute-start(f32[328,128]{1,0:T(8,128)S(1)} %get-tuple-element.69), channel_id=1, source_target_pairs={{0,4},{1,5},{2,6},{3,7},{4,0},{5,1},{6,2},{7,3},{8,12},{9,13},{10,... | collective-permute-start | bytes 503816 | tf_op jit(solution)/shard_map/ppermute | solution.py:359
  105.1 5.9 %collective-permute-start.23 = (f32[328,128]{1,0:T(8,128)S(1)}, f32[328,128]{1,0:T(8,128)S(1)}, u32[]{:S(2)}, u32[]{:S(2)}) collective-permute-start(f32[328,128]{1,0:T(8,128)S(1)} %fusion.19.rest_0_), channel_id=1, source_target_pairs={{0,2},{1,3},{2,4},{3,5},{4,6},{5,7},{6,0},{7,1},{8,10},{9,11},{10,... | collective-permute-start | bytes 503816 | tf_op jit(solution)/shard_map/ppermute | solution.py:359
  105.7 9.1 %collective-permute-start.22 = (f32[328,128]{1,0:T(8,128)S(1)}, f32[328,128]{1,0:T(8,128)S(1)}, u32[]{:S(2)}, u32[]{:S(2)}) collective-permute-start(f32[328,128]{1,0:T(8,128)S(1)} %fusion.19.rest_0_), channel_id=1, source_target_pairs={{0,4},{1,5},{2,6},{3,7},{4,0},{5,1},{6,2},{7,3},{8,12},{9,13},{10,... | collective-permute-start | bytes 503816 | tf_op jit(solution)/shard_map/ppermute | solution.py:359
  108.1 8.8 %collective-permute-start.21 = (f32[328,128]{1,0:T(8,128)S(1)}, f32[328,128]{1,0:T(8,128)S(1)}, u32[]{:S(2)}, u32[]{:S(2)}) collective-permute-start(f32[328,128]{1,0:T(8,128)S(1)} %fusion.19.rest_0_), channel_id=1, source_target_pairs={{0,6},{1,7},{2,0},{3,1},{4,2},{5,3},{6,4},{7,5},{8,14},{9,15},{10,... | collective-permute-start | bytes 503816 | tf_op jit(solution)/shard_map/ppermute | solution.py:359
  108.2 9.1 %collective-permute-start.24 = (f32[328,128]{1,0:T(8,128)S(1)}, f32[328,128]{1,0:T(8,128)S(1)}, u32[]{:S(2)}, u32[]{:S(2)}) collective-permute-start(f32[328,128]{1,0:T(8,128)S(1)} %fusion.19.rest_0_), channel_id=1, source_target_pairs={{0,1},{1,0},{2,3},{3,2},{4,5},{5,4},{6,7},{7,6},{8,9},{9,8},{10,11... | collective-permute-start | bytes 503816 | tf_op jit(solution)/shard_map/ppermute | solution.py:363
  110.9 6.3 %collective-permute-start.27 = (f32[328,128]{1,0:T(8,128)S(1)}, f32[328,128]{1,0:T(8,128)S(1)}, u32[]{:S(2)}, u32[]{:S(2)}) collective-permute-start(f32[328,128]{1,0:T(8,128)S(1)} %collective-permute-done.23.rest_3_), channel_id=1, source_target_pairs={{0,1},{1,0},{2,3},{3,2},{4,5},{5,4},{6,7},{7,6},{8,9},{9,8},{10,11... | collective-permute-start | bytes 503816 | tf_op jit(solution)/shard_map/ppermute | solution.py:363
  114.8 3.2 %collective-permute-start.26 = (f32[328,128]{1,0:T(8,128)S(1)}, f32[328,128]{1,0:T(8,128)S(1)}, u32[]{:S(2)}, u32[]{:S(2)}) collective-permute-start(f32[328,128]{1,0:T(8,128)S(1)} %collective-permute-done.22.rest_2_), channel_id=1, source_target_pairs={{0,1},{1,0},{2,3},{3,2},{4,5},{5,4},{6,7},{7,6},{8,9},{9,8},{10,11... | collective-permute-start | bytes 503816 | tf_op jit(solution)/shard_map/ppermute | solution.py:363
  117.0 1.4 %collective-permute-start.25 = (f32[328,128]{1,0:T(8,128)S(1)}, f32[328,128]{1,0:T(8,128)S(1)}, u32[]{:S(2)}, u32[]{:S(2)}) collective-permute-start(f32[328,128]{1,0:T(8,128)S(1)} %collective-permute-done.21.rest_1_), channel_id=1, source_target_pairs={{0,1},{1,0},{2,3},{3,2},{4,5},{5,4},{6,7},{7,6},{8,9},{9,8},{10,11... | collective-permute-start | bytes 503816 | tf_op jit(solution)/shard_map/ppermute | solution.py:363
